TPU v7x, 32 devices: a whole 2x2x4 slice. The times are simulated.
32 devices in a mesh: groups: 2 (over y), dp: 4 (over x, core), mp: 4 (over z).
Axes of the slice: x: 2, y: 2, z: 4, core: 2. Of those that a mesh axis runs over, the one named last changes fastest.
Arguments:
- hidden: bfloat16 [2, 16, 4, 8192], P(None, 'groups', 'dp', 'mp'), parts along dimension 1, may hold values from -60 to 60
- gain: float32 [8192], P('mp'), may hold values from 0.1 to 1.9
- w_query: bfloat16 [8192, 4096], P('mp'), may hold values from -0.0625 to 0.0625
- w_key: bfloat16 [8192, 512], P('mp'), may hold values from -0.1875 to 0.1875
- w_value: bfloat16 [8192, 512], P('mp'), may hold values from -0.0625 to 0.0625
- query_bias: float32 [4096], replicated, may hold values from -4 to 4
- key_bias: float32 [512], replicated, may hold values from -6 to 6
- value_bias: float32 [512], replicated, may hold values from -4 to 4
- w_out: bfloat16 [4096, 8192], P(None, 'mp'), may hold values from -0.09375 to 0.09375
- prompt_keys: bfloat16 [16, 32768, 512], P('groups', ('dp', 'mp')), parts along dimension 0, may hold values from -10 to 10
- prompt_values: bfloat16 [16, 32768, 512], P('groups', ('dp', 'mp')), parts along dimension 0, may hold values from -6 to 6
- gen_keys: bfloat16 [16, 4, 32, 512], P('groups', 'dp', 'mp'), parts along dimension 0, may hold values from -10 to 10
- gen_values: bfloat16 [16, 4, 32, 512], P('groups', 'dp', 'mp'), parts along dimension 0, may hold values from -6 to 6
- parents: int32 [2, 16, 4], P(None, 'groups'), parts along dimension 1, may hold values from 0 to 3
Outputs:
- attn_out: bfloat16 [2, 16, 4, 8192], P(None, 'groups', 'dp', 'mp'), parts along dimension 1
There are 2 independent parts, one for each index of `groups`. A program takes and returns all parts, laid end to end along the dimension named above; an argument that names none is the same for every part. Nothing has to cross between parts.
All inputs are finite; a program needn't handle non-finite values.
Results may differ from a plain program's by a relative error of at most 0.0098.
Values may be sent and summed in bfloat16 or wider, within the bound.
A program may use at most 192 MiB of HBM per device.

v0:
```python
import jax
import jax.numpy as jnp
from jax import lax
from jax.sharding import PartitionSpec as P

D = 8192
QH = 32
KVH = 4
HD = 128


negative_fill = -1e30


def project_local(hidden_rows, gain, w_query, w_key, w_value, query_bias, key_bias, value_bias):
    widened = hidden_rows.astype(jnp.float32)
    squares = jnp.sum(widened * widened, axis=-1)
    scaled = (widened * gain).astype(jnp.bfloat16)
    partial_query = jnp.dot(scaled, w_query, preferred_element_type=jnp.float32)
    partial_key = jnp.dot(scaled, w_key, preferred_element_type=jnp.float32)
    partial_value = jnp.dot(scaled, w_value, preferred_element_type=jnp.float32)
    partial_query, partial_key, partial_value, squares = lax.psum(
        (partial_query, partial_key, partial_value, squares), "mp"
    )
    inverse = lax.rsqrt(squares / D + 1e-06)[:, None]
    query = (partial_query * inverse + query_bias).astype(jnp.bfloat16)
    new_key = (partial_key * inverse + key_bias).astype(jnp.bfloat16)
    new_value = (partial_value * inverse + value_bias).astype(jnp.bfloat16)
    return (query, new_key, new_value)


def select_parent(array, parent):
    return jnp.take_along_axis(array, parent[:, :, None, None], axis=1)[:, 0]


def fork_caches(parents_step, beam_index, keys_now, values_now, history_keys, history_values):
    every_keys, every_values, every_hist_keys, every_hist_values = (
        lax.all_gather(keys_now[:, None], "dp", axis=1, tiled=True),
        lax.all_gather(values_now[:, None], "dp", axis=1, tiled=True),
        lax.all_gather(history_keys[:, None], "dp", axis=1, tiled=True),
        lax.all_gather(history_values[:, None], "dp", axis=1, tiled=True),
    )
    parent = lax.dynamic_slice_in_dim(parents_step, beam_index, 1, 1)
    return (
        select_parent(every_keys, parent),
        select_parent(every_values, parent),
        select_parent(every_hist_keys, parent),
        select_parent(every_hist_values, parent),
    )


def on_device(
    hidden,
    gain,
    w_query,
    w_key,
    w_value,
    query_bias,
    key_bias,
    value_bias,
    w_out,
    prompt_keys,
    prompt_values,
    gen_keys,
    gen_values,
    parents,
):
    beam_index = lax.axis_index("dp")
    model_index = lax.axis_index("mp")
    beam_count = lax.axis_size("dp")
    step_count = hidden.shape[0]
    prompt_count = hidden.shape[1]
    repeat = QH // KVH
    score_factor = HD ** (-0.5)
    leader = model_index == 0
    beam_ids = jnp.arange(beam_count, dtype=jnp.int32)
    own_beam = jnp.broadcast_to((beam_ids == beam_index)[None, :], (prompt_count, beam_count))
    prompt_k = prompt_keys.reshape(prompt_count, -1, KVH, HD)
    prompt_v = prompt_values.reshape(prompt_count, -1, KVH, HD)
    current_keys = gen_keys[:, 0]
    current_values = gen_values[:, 0]
    gen_width = current_keys.shape[1]
    history_keys = jnp.zeros((prompt_count, step_count, KVH * HD), jnp.bfloat16)
    history_values = jnp.zeros((prompt_count, step_count, KVH * HD), jnp.bfloat16)
    outputs = []
    for step in range(step_count):
        query, new_key, new_value = project_local(
            hidden[step][:, 0], gain, w_query, w_key, w_value, query_bias, key_bias, value_bias
        )
        gathered = lax.all_gather(query[:, None], "dp", axis=1, tiled=True)
        grouped = gathered.reshape(prompt_count, beam_count, KVH, repeat, HD)
        history_seen = []
        current_keys, current_values, history_keys, history_values = fork_caches(
            parents[step], beam_index, current_keys, current_values, history_keys, history_values
        )
        for earlier in range(step):
            history_seen.append(own_beam & leader)
        seen_parts = [jnp.broadcast_to(own_beam[:, :, None], (prompt_count, beam_count, gen_width))]
        seen_parts = seen_parts + [flag[:, :, None] for flag in history_seen]
        seen_parts.append((own_beam & leader)[:, :, None])
        visible = jnp.concatenate(seen_parts, axis=2)
        keys_extra = jnp.concatenate(
            [current_keys, history_keys[:, :step], new_key[:, None]], axis=1
        )
        values_extra = jnp.concatenate(
            [current_values, history_values[:, :step], new_value[:, None]], axis=1
        )
        keys_extra = keys_extra.reshape(prompt_count, -1, KVH, HD)
        values_extra = values_extra.reshape(prompt_count, -1, KVH, HD)
        prompt_scores = (
            jnp.einsum("pbgrd,plgd->pbgrl", grouped, prompt_k, preferred_element_type=jnp.float32)
            * score_factor
        )
        extra_scores = (
            jnp.einsum("pbgrd,pngd->pbgrn", grouped, keys_extra, preferred_element_type=jnp.float32)
            * score_factor
        )
        visible_mask = visible[:, :, None, None, :]
        extra_scores = jnp.where(visible_mask, extra_scores, negative_fill)
        local_top = jnp.maximum(jnp.max(prompt_scores, axis=-1), jnp.max(extra_scores, axis=-1))
        top = lax.pmax(local_top, ("dp", "mp"))
        prompt_weights = jnp.exp(prompt_scores - top[..., None]).astype(jnp.bfloat16)
        extra_weights = jnp.where(visible_mask, jnp.exp(extra_scores - top[..., None]), 0.0).astype(
            jnp.bfloat16
        )
        total = jnp.sum(prompt_weights, axis=-1, dtype=jnp.float32) + jnp.sum(
            extra_weights, axis=-1, dtype=jnp.float32
        )
        numerator = jnp.einsum(
            "pbgrl,plgd->pbgrd", prompt_weights, prompt_v, preferred_element_type=jnp.float32
        )
        numerator = numerator + jnp.einsum(
            "pbgrn,pngd->pbgrd", extra_weights, values_extra, preferred_element_type=jnp.float32
        )
        numerator, total = lax.psum((numerator, total), ("dp", "mp"))
        numerator = lax.dynamic_slice_in_dim(numerator, beam_index, 1, 1)
        total = lax.dynamic_slice_in_dim(total, beam_index, 1, 1)
        attended = (
            (numerator / total[..., None]).reshape(prompt_count, QH * HD).astype(jnp.bfloat16)
        )
        result = jnp.dot(attended, w_out, preferred_element_type=jnp.float32).astype(jnp.bfloat16)
        outputs.append(result[:, None])
        history_keys = history_keys.at[:, step].set(new_key)
        history_values = history_values.at[:, step].set(new_value)
    return jnp.stack(outputs)


def solution(mesh):
    return jax.shard_map(
        on_device,
        mesh=mesh,
        in_specs=(
            P(None, "groups", "dp", "mp"),
            P("mp"),
            P("mp", None),
            P("mp", None),
            P("mp", None),
            P(),
            P(),
            P(),
            P(None, "mp"),
            P("groups", ("dp", "mp"), None),
            P("groups", ("dp", "mp"), None),
            P("groups", "dp", "mp", None),
            P("groups", "dp", "mp", None),
            P(None, "groups", None),
        ),
        out_specs=P(None, "groups", "dp", "mp"),
        check_vma=False,
    )
```

profile of v0, /device:TPU:0, one launch (start us, length us, event | category | flops | bytes accessed | tf_op | source)
XLA Modules:
  0.0 379.4 jit_solution(4389123546313905021)
XLA Ops:
  6.5 1.6 fusion.45
  8.2 1.8 fusion.60
  9.9 1.8 fusion.66
  11.7 2.6 fusion.58
  14.3 2.6 fusion.64
  17.0 8.8 %fusion.62 = f32[8,4096]{1,0:T(8,128)} fusion(bf16[2048,4096]{1,0:T(8,128)(2,1)} %param.24, f32[2048]{0:T(1024)S(1)} %copy-done.4, bf16[2,8,1,2048]{3,1,2,0:T(8,128)(2,1)S(1)} %copy-done.3), kind=kOutput, calls=%fused_computation.103 | convolution fusion | flops 134266880 | bytes 16949248 | tf_op jit(solution)/shard_map/dot_general | solution.py:19
  25.8 1.8 copy-done.2
  27.6 2.9 fusion.68
  31.9 7.2 %all_gather.29 = bf16[8,4,8,512]{3,2,1,0:T(8,128)(2,1)S(1)} all-gather(bf16[8,1,8,512]{3,2,1,0:T(8,128)(2,1)S(1)} %copy-done.5), channel_id=1, replica_groups=mesh['groups'=2,'dp'=4,'mp'=4] {'dp'}, dimensions={1}, use_global_device_ids=true | all-gather | bytes 327680 | tf_op jit(solution)/shard_map/all_gather | solution.py:38
  39.6 5.9 %all_gather.30 = bf16[8,4,8,512]{3,2,1,0:T(8,128)(2,1)S(1)} all-gather(bf16[8,1,8,512]{3,2,1,0:T(8,128)(2,1)S(1)} %copy-done.6), channel_id=1, replica_groups=mesh['groups'=2,'dp'=4,'mp'=4] {'dp'}, dimensions={1}, use_global_device_ids=true | all-gather | bytes 327680 | tf_op jit(solution)/shard_map/all_gather | solution.py:39
  46.2 5.9 %all_gather.35 = bf16[8,4,8,512]{3,2,0,1:T(8,128)(2,1)S(1)} all-gather(bf16[8,1,8,512]{3,2,0,1:T(8,128)(2,1)S(1)} %get-tuple-element.62), channel_id=1, replica_groups=mesh['groups'=2,'dp'=4,'mp'=4] {'dp'}, dimensions={1}, use_global_device_ids=true | all-gather | bytes 327680 | tf_op jit(solution)/shard_map/all_gather | solution.py:39
  52.0 5.8 %all_gather.32 = bf16[8,4,8,512]{3,2,0,1:T(8,128)(2,1)S(1)} all-gather(bf16[8,1,8,512]{3,2,0,1:T(8,128)(2,1)S(1)} %get-tuple-element.63), channel_id=1, replica_groups=mesh['groups'=2,'dp'=4,'mp'=4] {'dp'}, dimensions={1}, use_global_device_ids=true | all-gather | bytes 327680 | tf_op jit(solution)/shard_map/all_gather | solution.py:38
  59.0 23.7 %reshape.196 = bf16[8,2048,4,128]{3,2,1,0:T(4,128)(2,1)} reshape(bf16[8,2048,512]{2,1,0:T(8,128)(2,1)} %param.31) | data formatting | bytes 33554432 | tf_op jit(solution)/shard_map/reshape | solution.py:78
  82.8 23.8 %reshape.197 = bf16[8,2048,4,128]{3,2,1,0:T(4,128)(2,1)} reshape(bf16[8,2048,512]{2,1,0:T(8,128)(2,1)} %param.32) | data formatting | bytes 33554432 | tf_op jit(solution)/shard_map/reshape | solution.py:79
  108.3 5.2 %all_gather.36 = bf16[8,4,2,512]{3,0,2,1:T(8,128)(2,1)S(1)} all-gather(bf16[8,1,2,512]{3,0,2,1:T(8,128)(2,1)S(1)} %copy.64), channel_id=1, replica_groups=mesh['groups'=2,'dp'=4,'mp'=4] {'dp'}, dimensions={1}, use_global_device_ids=true | all-gather | bytes 81920 | tf_op jit(solution)/shard_map/all_gather | solution.py:41
  114.4 5.2 %all_gather.34 = bf16[8,4,2,512]{3,0,2,1:T(8,128)(2,1)S(1)} all-gather(bf16[8,1,2,512]{3,0,2,1:T(8,128)(2,1)S(1)} %copy.56), channel_id=1, replica_groups=mesh['groups'=2,'dp'=4,'mp'=4] {'dp'}, dimensions={1}, use_global_device_ids=true | all-gather | bytes 81920 | tf_op jit(solution)/shard_map/all_gather | solution.py:40
  120.5 1.1 add_convert_fusion.1
  121.6 5.9 %all-gather = bf16[8,16384]{1,0:T(8,128)(2,1)S(1)} all-gather(bf16[8,4096]{1,0:T(8,128)(2,1)S(1)} %get-tuple-element.51), channel_id=2, replica_groups=mesh['groups'=2,'dp'=4,'mp'=4] {'dp'}, dimensions={1}, use_global_device_ids=true | all-gather | bytes 327680 | tf_op jit(solution)/shard_map/all_gather | solution.py:90
  127.5 6.0 %all-gather.1 = bf16[8,16384]{1,0:T(8,128)(2,1)S(1)} all-gather(bf16[8,4096]{1,0:T(8,128)(2,1)S(1)} %get-tuple-element.52), channel_id=3, replica_groups=mesh['groups'=2,'dp'=4,'mp'=4] {'dp'}, dimensions={1}, use_global_device_ids=true | all-gather | bytes 327680 | tf_op jit(solution)/shard_map/all_gather | solution.py:90
  133.5 14.5 %bitcast_reduce_fusion = (f32[8,4,4,8]{3,1,2,0:T(4,128)S(1)}, f32[8,4,4,8,2048]{4,3,2,1,0:T(8,128)}) fusion(bf16[8,2048,4,128,1]{3,2,1,0,4:T(4,128)(2,1)} %bitcast.216, bf16[8,4,4,8,128]{4,0,3,2,1:T(8,128)(2,1)S(1)} %bitcast.220), kind=kOutput, calls=%fused_computation.16 | convolution fusion | flops 541064192 | bytes 25432064 | tf_op jit(solution)/shard_map/pbgrd,plgd->pbgrl/dot_general | solution.py:111
  148.0 14.5 %bitcast_reduce_fusion.1 = (f32[8,4,4,8]{3,1,2,0:T(4,128)S(1)}, f32[8,4,4,8,2048]{4,3,2,1,0:T(8,128)}) fusion(bf16[8,2048,4,128,1]{3,2,1,0,4:T(4,128)(2,1)} %bitcast.217, bf16[8,4,4,8,128]{4,0,3,2,1:T(8,128)(2,1)S(1)} %bitcast.222), kind=kOutput, calls=%fused_computation.20 | convolution fusion | flops 541064192 | bytes 25432064 | tf_op jit(solution)/shard_map/pbgrd,plgd->pbgrl/dot_general | solution.py:111
  163.3 63.8 %all-reduce.2 = (f32[8,4,4,8]{3,1,2,0:T(4,128)S(1)}, f32[8,4,4,8]{3,1,2,0:T(4,128)S(1)}) all-reduce(f32[8,4,4,8]{3,1,2,0:T(4,128)S(1)} %max.11, f32[8,4,4,8]{3,1,2,0:T(4,128)S(1)} %max.10), channel_id=1, replica_groups=mesh['groups'=2,'dp'=4,'mp'=4] {'dp','mp'}, use_global_device_ids=true, to_apply=%region_18.21 | all-reduce | flops 2048 | bytes 16384 | tf_op jit(solution)/shard_map/pmax | solution.py:121
  227.1 4.3 %convert_reduce_fusion = f32[8,4,4,8]{3,1,2,0:T(4,128)S(1)} fusion(f32[8,4,4,8]{3,1,2,0:T(4,128)S(1)} %get-tuple-element.37, f32[8,4,4,8,2048]{4,3,2,1,0:T(8,128)} %get-tuple-element.69), kind=kLoop, calls=%fused_computation.23 | loop fusion | flops 10484736 | bytes 8396800 | tf_op jit(solution)/shard_map/reduce_sum | solution.py:126
  231.5 12.1 %fusion.23 = f32[8,4,4,8,128]{4,3,1,2,0:T(8,128)S(1)} fusion(bf16[8,2048,4,128,1]{3,2,1,0,4:T(4,128)(2,1)} %bitcast.218, f32[8,4,4,8,2048]{4,3,2,1,0:T(8,128)} %get-tuple-element.69, f32[8,4,4,8]{3,1,2,0:T(4,128)S(1)} %get-tuple-element.37), kind=kOutput, calls=%fused_computation.40 | convolution fusion | flops 543162368 | bytes 25694208 | tf_op jit(solution)/shard_map/pbgrl,plgd->pbgrd/dot_general | solution.py:129
  243.6 4.3 %convert_reduce_fusion.1 = f32[8,4,4,8]{3,1,2,0:T(4,128)S(1)} fusion(f32[8,4,4,8]{3,1,2,0:T(4,128)S(1)} %get-tuple-element.38, f32[8,4,4,8,2048]{4,3,2,1,0:T(8,128)} %get-tuple-element.73), kind=kLoop, calls=%fused_computation.24 | loop fusion | flops 10484736 | bytes 8396800 | tf_op jit(solution)/shard_map/reduce_sum | solution.py:126
  247.9 12.1 %fusion.20 = f32[8,4,4,8,128]{4,3,1,2,0:T(8,128)S(1)} fusion(bf16[8,2048,4,128,1]{3,2,1,0,4:T(4,128)(2,1)} %bitcast.219, f32[8,4,4,8,2048]{4,3,2,1,0:T(8,128)} %get-tuple-element.73, f32[8,4,4,8]{3,1,2,0:T(4,128)S(1)} %get-tuple-element.38), kind=kOutput, calls=%fused_computation.39 | convolution fusion | flops 543162368 | bytes 25694208 | tf_op jit(solution)/shard_map/pbgrl,plgd->pbgrd/dot_general | solution.py:129
  260.1 1.1 fusion.14
  261.2 1.1 fusion.15
  263.4 60.2 %all-reduce = (f32[8,4,4,8]{3,1,2,0:T(4,128)S(1)}, f32[8,4,4,8]{3,1,2,0:T(4,128)S(1)}) all-reduce(f32[8,4,4,8]{3,1,2,0:T(4,128)S(1)} %add.117, f32[8,4,4,8]{3,1,2,0:T(4,128)S(1)} %add.111), channel_id=1, replica_groups=mesh['groups'=2,'dp'=4,'mp'=4] {'dp','mp'}, use_global_device_ids=true, to_apply=%region_23.26 | all-reduce | flops 2048 | bytes 16384 | tf_op jit(solution)/shard_map/psum | solution.py:135
  323.6 30.3 %all-reduce.9.cloned.1.call-done = (f32[8,4,4,8,128]{4,3,1,2,0:T(8,128)}, f32[8,4,4,8,128]{4,3,1,2,0:T(8,128)}) async-done(((f32[8,4,4,8,128]{4,3,1,2,0:T(8,128)}, f32[8,4,4,8,128]{4,3,1,2,0:T(8,128)}), (f32[8,4,4,8,128]{4,3,1,2,0:T(8,128)}, f32[8,4,4,8,128]{4,3,1,2,0:T(8,128)})) %all-reduce.9.cloned.1.call-update) | async-done | bytes 1048592 | tf_op jit(solution)/shard_map/psum | solution.py:135
  356.0 8.2 %fusion.12 = bf16[1,8,1,2048]{3,1,2,0:T(8,128)(2,1)S(1)} fusion(bf16[4096,2048]{1,0:T(8,128)(2,1)} %param.30, bf16[1,8,32,128]{3,2,1,0:T(8,128)(2,1)S(1)} %fusion.54), kind=kOutput, calls=%fused_computation.27 | convolution fusion | flops 134234112 | bytes 16875520 | tf_op jit(solution)/shard_map/dot_general | solution.py:141
  364.2 8.1 %fusion.13 = bf16[1,8,1,2048]{3,1,2,0:T(8,128)(2,1)S(1)} fusion(bf16[4096,2048]{1,0:T(8,128)(2,1)} %param.30, bf16[1,8,32,128]{3,2,1,0:T(8,128)(2,1)S(1)} %fusion.55), kind=kOutput, calls=%fused_computation.28 | convolution fusion | flops 134234112 | bytes 16875520 | tf_op jit(solution)/shard_map/dot_general | solution.py:141
  (87 shorter events, 11.5 us)
Async XLA Ops:
  6.5 1.6 copy-start
  6.5 10.4 %copy-start.3 = (bf16[2,8,1,2048]{3,1,2,0:T(8,128)(2,1)S(1)}, bf16[2,8,1,2048]{3,1,2,0:T(8,128)(2,1)}, u32[]{:S(2)}) copy-start(bf16[2,8,1,2048]{3,1,2,0:T(8,128)(2,1)} %param.22) | copy-start | bytes 196612
  6.5 10.4 %copy-start.4 = (f32[2048]{0:T(1024)S(1)}, f32[2048]{0:T(1024)}, u32[]{:S(2)}) copy-start(f32[2048]{0:T(1024)} %param.23) | copy-start | bytes 24580
  6.5 100.1 %all-reduce.11.cloned.1.call-start = ((), (), s32[]{:S(2)}) async-start(), calls=%async_computation.1 | async-start | bytes 133120 | tf_op jit(solution)/shard_map/psum | solution.py:22
  16.9 103.6 %all-reduce.13.cloned.1.call-start = ((), (), s32[]{:S(2)}) async-start(), calls=%async_computation.2 | async-start | bytes 524288 | tf_op jit(solution)/shard_map/psum | solution.py:22
  17.0 10.6 %copy-start.2 = (bf16[2048,4096]{1,0:T(8,128)(2,1)S(1)}, bf16[2048,4096]{1,0:T(8,128)(2,1)}, u32[]{:S(2)}) copy-start(bf16[2048,4096]{1,0:T(8,128)(2,1)} %param.24) | copy-start | bytes 50331652
  27.6 3.4 copy-start.8
  27.6 4.3 %copy-start.5 = (bf16[8,1,8,512]{3,2,1,0:T(8,128)(2,1)S(1)}, bf16[8,1,8,512]{3,2,1,0:T(8,128)(2,1)}, u32[]{:S(2)}) copy-start(bf16[8,1,8,512]{3,2,1,0:T(8,128)(2,1)} %param.33) | copy-start | bytes 196612
  27.6 12.0 %copy-start.6 = (bf16[8,1,8,512]{3,2,1,0:T(8,128)(2,1)S(1)}, bf16[8,1,8,512]{3,2,1,0:T(8,128)(2,1)}, u32[]{:S(2)}) copy-start(bf16[8,1,8,512]{3,2,1,0:T(8,128)(2,1)} %param.34) | copy-start | bytes 196612
  30.6 323.4 %all-reduce.9.cloned.1.call-start = ((), (), s32[]{:S(2)}) async-start(), calls=%async_computation | async-start | bytes 2097152 | tf_op jit(solution)/shard_map/psum | solution.py:135
  82.8 24.6 %copy-start.9 = (f32[512]{0:T(512)S(1)}, f32[512]{0:T(512)}, u32[]{:S(2)}) copy-start(f32[512]{0:T(512)} %param.28) | copy-start | bytes 6148
  82.8 24.6 %copy-start.10 = (f32[512]{0:T(512)S(1)}, f32[512]{0:T(512)}, u32[]{:S(2)}) copy-start(f32[512]{0:T(512)} %param.29) | copy-start | bytes 6148
  82.8 37.8 %copy-start.7 = (f32[4096]{0:T(1024)S(1)}, f32[4096]{0:T(1024)}, u32[]{:S(2)}) copy-start(f32[4096]{0:T(1024)} %param.27) | copy-start | bytes 49156
  356.0 16.9 %copy-start.1 = (bf16[2048,512]{1,0:T(8,128)(2,1)S(1)}, bf16[2048,512]{1,0:T(8,128)(2,1)}, u32[]{:S(2)}) copy-start(bf16[2048,512]{1,0:T(8,128)(2,1)} %param.25) | copy-start | bytes 6291460
Sparse Core Ops, SparseCore 0:
  17.0 37.3 all-reduce.10
  56.9 35.5 all-reduce.12
  262.5 91.3 all-reduce.8
where the time goes:
time: 381 us; the launch traced here: 379 us
  blocking collectives  171 us (45%)
  matrix products  93 us (24%)
  local copies, waits for them, and re-layouts  54.1 us (14%)
  waiting for transfers between devices  30.4 us (8%)
  other arithmetic  17.1 us (4%)
  between operations  13.6 us (4%)
    pmax x1, blocking collectives, on_device(): top = lax.pmax(local_top, ('dp', 'mp'))  63.8 us
    psum x1, blocking collectives, on_device(): numerator, total = lax.psum((numerator, total), ('dp', 'mp'))  60.2 us
    psum x1, waiting for transfers between devices, on_device(): numerator, total = lax.psum((numerator, total), ('dp', 'mp'))  30.3 us
    dot_general x2, matrix products, on_device(): jnp.einsum('pbgrd,plgd->pbgrl', grouped, prompt_k, preferred_element_type...  29 us
    dot_general x2, matrix products, on_device(): jnp.einsum('pbgrl,plgd->pbgrd', prompt_weights, prompt_v, preferred_eleme...  24.3 us
    reshape x1, local copies, waits for them, and re-layouts, on_device(): prompt_v = prompt_values.reshape(prompt_count, -1, KVH, HD)  23.8 us
    reshape x1, local copies, waits for them, and re-layouts, on_device(): prompt_k = prompt_keys.reshape(prompt_count, -1, KVH, HD)  23.7 us
    dot_general x2, matrix products, on_device(): jnp.dot(attended, w_out, preferred_element_type=jnp.float32)  16.2 us
  transfers between devices with their start and end apart: 3, of which 1 were waited for; matrix products, arithmetic and copies ran while one was open for 18% of the time, Pallas kernels for 0%

commit v1 on v0

v1 whole, which is shorter than its diff:
```python
import functools

import jax
import jax.numpy as jnp
from jax import lax
from jax.experimental import pallas as pl
from jax.experimental.pallas import tpu as pltpu
from jax.sharding import PartitionSpec as P

D = 8192
QH = 32
KVH = 4
HD = 128
REPEAT = QH // KVH
HEADS = QH + 2 * KVH
MESH = pl.DeviceIdType.MESH
VMEM_LIMIT = 48 * 1024 * 1024
hidden_fill = -1e30


def exchange_kernel(
    dp_count,
    mp_count,
    per_rank,
    query_ref,
    key_ref,
    value_ref,
    squares_ref,
    bias_ref,
    out_ref,
    parts,
    landed,
    gathered,
    reduce_send,
    reduce_recv,
    spread_send,
    spread_recv,
    far_send,
    far_recv,
    near_send,
    near_recv,
):
    beam = lax.axis_index("dp")
    rank = lax.axis_index("mp")
    rows = squares_ref.shape[0]
    far = lax.rem(beam + dp_count // 2, dp_count)
    near = beam + 1 - 2 * lax.rem(beam, 2)

    barrier = pltpu.get_barrier_semaphore()
    for delta in range(1, mp_count):
        pl.semaphore_signal(
            barrier,
            inc=1,
            device_id={"mp": lax.rem(rank + delta, mp_count)},
            device_id_type=MESH,
        )
    for partner in (far, near):
        pl.semaphore_signal(barrier, inc=1, device_id={"dp": partner}, device_id_type=MESH)

    for owner in range(mp_count):
        for place in range(per_rank):
            head = owner * per_rank + place
            if head < QH:
                part = query_ref[:, head * HD : (head + 1) * HD]
            elif head < QH + KVH:
                part = key_ref[:, (head - QH) * HD : (head - QH + 1) * HD]
            elif head < HEADS:
                first = (head - QH - KVH) * HD
                part = value_ref[:, first : first + HD]
            else:
                part = jnp.zeros((rows, HD), jnp.float32)
            parts[owner, place] = part
        parts[owner, per_rank] = squares_ref[...]
    pl.semaphore_wait(barrier, mp_count + 1)

    def reduce_copy(delta):
        peer = lax.rem(rank + delta, mp_count)
        return pltpu.make_async_remote_copy(
            src_ref=parts.at[peer],
            dst_ref=landed.at[delta],
            send_sem=reduce_send.at[delta],
            recv_sem=reduce_recv.at[delta],
            device_id={"mp": peer},
            device_id_type=MESH,
        )

    for delta in range(1, mp_count):
        reduce_copy(delta).start()
    total = parts[rank]
    for delta in range(1, mp_count):
        reduce_copy(delta).wait_recv()
        total = total + landed[delta]
    inverse = lax.rsqrt(total[per_rank] / D + 1e-06)
    mine = pl.ds(rank * per_rank, per_rank)
    done = total[:per_rank] * inverse[None] + bias_ref[mine][:, None, :]
    gathered[beam, mine] = done.astype(jnp.bfloat16)

    def spread_copy(delta):
        peer = lax.rem(rank + delta, mp_count)
        return pltpu.make_async_remote_copy(
            src_ref=gathered.at[beam, mine],
            dst_ref=gathered.at[beam, mine],
            send_sem=spread_send.at[delta],
            recv_sem=spread_recv.at[delta],
            device_id={"mp": peer},
            device_id_type=MESH,
        )

    def dp_copy(delta, source_beam, partner, send, recv, slot):
        owner = lax.rem(rank - delta + mp_count, mp_count)
        block = pl.ds(owner * per_rank, per_rank)
        return pltpu.make_async_remote_copy(
            src_ref=gathered.at[source_beam, block],
            dst_ref=gathered.at[source_beam, block],
            send_sem=send.at[slot, delta],
            recv_sem=recv.at[slot, delta],
            device_id={"dp": partner},
            device_id_type=MESH,
        )

    for delta in range(1, mp_count):
        spread_copy(delta).start()
    for delta in range(mp_count):
        if delta:
            spread_copy(delta).wait_recv()
        dp_copy(delta, beam, far, far_send, far_recv, 0).start()
        dp_copy(delta, beam, near, near_send, near_recv, 0).start()
    for delta in range(mp_count):
        dp_copy(delta, beam, far, far_send, far_recv, 0).wait_recv()
        dp_copy(delta, far, near, near_send, near_recv, 1).start()
    for delta in range(mp_count):
        dp_copy(delta, beam, near, near_send, near_recv, 0).wait_recv()
        dp_copy(delta, far, near, near_send, near_recv, 1).wait_recv()
    for delta in range(mp_count):
        if delta:
            reduce_copy(delta).wait_send()
            spread_copy(delta).wait_send()
        dp_copy(delta, beam, far, far_send, far_recv, 0).wait_send()
        dp_copy(delta, beam, near, near_send, near_recv, 0).wait_send()
        dp_copy(delta, far, near, near_send, near_recv, 1).wait_send()
    out_ref[...] = gathered[...]


def exchange(query, key, value, squares, bias, dp_count, mp_count, per_rank):
    rows = squares.shape[0]
    heads = mp_count * per_rank
    vmem = pl.BlockSpec(memory_space=pltpu.VMEM)
    dma = pltpu.SemaphoreType.DMA
    return pl.pallas_call(
        functools.partial(exchange_kernel, dp_count, mp_count, per_rank),
        out_shape=jax.ShapeDtypeStruct((dp_count, heads, rows, HD), jnp.bfloat16),
        in_specs=[vmem] * 5,
        out_specs=vmem,
        scratch_shapes=[
            pltpu.VMEM((mp_count, per_rank + 1, rows, HD), jnp.float32),
            pltpu.VMEM((mp_count, per_rank + 1, rows, HD), jnp.float32),
            pltpu.VMEM((dp_count, heads, rows, HD), jnp.bfloat16),
            dma((mp_count,)),
            dma((mp_count,)),
            dma((mp_count,)),
            dma((mp_count,)),
            dma((1, mp_count)),
            dma((1, mp_count)),
            dma((2, mp_count)),
            dma((2, mp_count)),
        ],
        compiler_params=pltpu.CompilerParams(
            collective_id=0, has_side_effects=True, vmem_limit_bytes=VMEM_LIMIT
        ),
        name="exchange",
    )(query, key, value, squares, bias)


def attend_kernel(
    query_ref, key_ref, value_ref, extra_key_ref, extra_value_ref, mask_ref, out_ref, stat_ref
):
    pair = pl.program_id(1)
    factor = HD ** (-0.5)
    contract_last = (((1,), (1,)), ((), ()))
    query = query_ref[0, 0]
    rows = query.shape[0]
    scores = lax.dot_general(
        query, key_ref[0], contract_last, preferred_element_type=jnp.float32
    )
    extra = lax.dot_general(
        query, extra_key_ref[0], contract_last, preferred_element_type=jnp.float32
    )
    extra = extra + mask_ref[0]
    top = jnp.maximum(
        jnp.max(scores, axis=-1, keepdims=True), jnp.max(extra, axis=-1, keepdims=True)
    )
    weights = jnp.exp((scores - top) * factor)
    extra_weights = jnp.exp((extra - top) * factor)
    total = jnp.sum(weights, axis=-1, keepdims=True) + jnp.sum(
        extra_weights, axis=-1, keepdims=True
    )
    numerator = jnp.dot(
        weights.astype(jnp.bfloat16), value_ref[0], preferred_element_type=jnp.float32
    ) + jnp.dot(
        extra_weights.astype(jnp.bfloat16), extra_value_ref[0], preferred_element_type=jnp.float32
    )
    row = lax.broadcasted_iota(jnp.int32, (rows, HD), 0)
    second = lax.rem(row // (rows // 8), 2) == 1
    own = jnp.where(second, numerator[:, HD:], numerator[:, :HD])
    out_ref[0, 0] = (own / total).astype(jnp.bfloat16)
    level = top * factor + jnp.log(total)
    flat = jnp.transpose(jnp.broadcast_to(level, (rows, HD)))
    stat_ref[0, pl.ds(pair, 1), :] = flat[:1]


def attend(query, prompt_keys, prompt_values, extra_keys, extra_values, mask):
    prompts, pairs, rows, wide = query.shape
    length = prompt_keys.shape[1]
    extras = extra_keys.shape[1]
    return pl.pallas_call(
        attend_kernel,
        grid=(prompts, pairs),
        out_shape=(
            jax.ShapeDtypeStruct((prompts, pairs, rows, HD), jnp.bfloat16),
            jax.ShapeDtypeStruct((prompts, 8, rows), jnp.float32),
        ),
        in_specs=[
            pl.BlockSpec((1, 1, rows, wide), lambda p, h: (p, h, 0, 0)),
            pl.BlockSpec((1, length, wide), lambda p, h: (p, 0, h)),
            pl.BlockSpec((1, length, wide), lambda p, h: (p, 0, h)),
            pl.BlockSpec((1, extras, wide), lambda p, h: (p, 0, h)),
            pl.BlockSpec((1, extras, wide), lambda p, h: (p, 0, h)),
            pl.BlockSpec((1, rows, extras), lambda p, h: (p, 0, 0)),
        ],
        out_specs=(
            pl.BlockSpec((1, 1, rows, HD), lambda p, h: (p, h, 0, 0)),
            pl.BlockSpec((1, 8, rows), lambda p, h: (p, 0, 0)),
        ),
        compiler_params=pltpu.CompilerParams(vmem_limit_bytes=VMEM_LIMIT),
        name="attend",
    )(query, prompt_keys, prompt_values, extra_keys, extra_values, mask)


def region(rank, prompts, mp_count):
    if mp_count <= prompts:
        each = prompts // mp_count
        return rank * each, each, 0, 2, 0, 32
    share = mp_count // prompts
    place = lax.rem(rank, share)
    if share == 2:
        return rank // share, 1, place, 1, 0, 32
    return rank // share, 1, place // 2, 1, lax.rem(place, 2) * 16, 16


def combine_kernel(
    dp_count,
    mp_count,
    out_in,
    stat_in,
    out_ref,
    outs,
    stats,
    landed,
    landed_stats,
    flipped,
    gathered,
    out_send,
    out_recv,
    stat_send,
    stat_recv,
    spread_send,
    spread_recv,
):
    beam = lax.axis_index("dp")
    rank = lax.axis_index("mp")
    count = dp_count * mp_count
    me = beam * mp_count + rank
    prompts = out_in.shape[0]
    beam_rows = out_in.shape[2] // dp_count

    barrier = pltpu.get_barrier_semaphore()

    def greet(delta, carry):
        peer = lax.rem(me + delta, count)
        pl.semaphore_signal(
            barrier,
            inc=1,
            device_id={"dp": peer // mp_count, "mp": lax.rem(peer, mp_count)},
            device_id_type=MESH,
        )
        return carry

    lax.fori_loop(1, count, greet, 0)
    outs[...] = out_in[...]
    stats[...] = stat_in[...]
    pl.semaphore_wait(barrier, count - 1)

    def views(peer):
        first, each, pair, pairs, row, rows = region(lax.rem(peer, mp_count), prompts, mp_count)
        start = pl.multiple_of((peer // mp_count) * beam_rows + row, 16)
        return (
            outs.at[pl.ds(first, each), pl.ds(pair, pairs), pl.ds(start, rows)],
            stats.at[pl.ds(first, each)],
        )

    def copies(delta):
        peer = lax.rem(me + delta, count)
        target = {"dp": peer // mp_count, "mp": lax.rem(peer, mp_count)}
        out_view, stat_view = views(peer)
        return (
            pltpu.make_async_remote_copy(
                src_ref=out_view,
                dst_ref=landed.at[delta],
                send_sem=out_send.at[delta],
                recv_sem=out_recv.at[delta],
                device_id=target,
                device_id_type=MESH,
            ),
            pltpu.make_async_remote_copy(
                src_ref=stat_view,
                dst_ref=landed_stats.at[delta],
                send_sem=stat_send.at[delta],
                recv_sem=stat_recv.at[delta],
                device_id=target,
                device_id_type=MESH,
            ),
        )

    def begin(delta, carry):
        for copy in copies(delta):
            copy.start()
        return carry

    def finish(delta, carry):
        for copy in copies(delta):
            copy.wait()
        return carry

    lax.fori_loop(1, count, begin, 0)
    first, each, pair, pairs, row, rows = region(rank, prompts, mp_count)
    start = pl.multiple_of(beam * beam_rows + row, 16)
    landed[0] = outs[pl.ds(first, each), pl.ds(pair, pairs), pl.ds(start, rows)]
    landed_stats[0] = stats[pl.ds(first, each)]
    lax.fori_loop(1, count, finish, 0)

    for item in range(each):
        levels = landed_stats[:, item]
        top = jnp.max(levels, axis=0, keepdims=True)
        shares = jnp.exp(levels - top)
        shares = shares / jnp.sum(shares, axis=0, keepdims=True)
        flipped[...] = jnp.transpose(shares.reshape(count * 8, shares.shape[-1]))
        columns = flipped[pl.ds(start, rows), :]
        for place in range(pairs):
            total = jnp.zeros((rows, HD), jnp.float32)
            for source in range(count):
                if pairs == 2:
                    column = columns[:, source * 8 + place : source * 8 + place + 1]
                else:
                    column = jnp.where(
                        pair == 1,
                        columns[:, source * 8 + 1 : source * 8 + 2],
                        columns[:, source * 8 : source * 8 + 1],
                    )
                total = total + column * landed[source, item, place].astype(jnp.float32)
            gathered[first + item, pair + place, pl.ds(pl.multiple_of(row, 16), rows)] = (
                total.astype(jnp.bfloat16)
            )

    def spread(delta):
        peer = lax.rem(rank + delta, mp_count)
        view = gathered.at[
            pl.ds(first, each), pl.ds(pair, pairs), pl.ds(pl.multiple_of(row, 16), rows)
        ]
        return pltpu.make_async_remote_copy(
            src_ref=view,
            dst_ref=view,
            send_sem=spread_send.at[delta],
            recv_sem=spread_recv.at[delta],
            device_id={"mp": peer},
            device_id_type=MESH,
        )

    for delta in range(1, mp_count):
        spread(delta).start()
    for delta in range(1, mp_count):
        spread(delta).wait()
    out_ref[...] = gathered[...]


def combine(outs, stats, dp_count, mp_count):
    prompts, pairs, rows, _ = outs.shape
    count = dp_count * mp_count
    _, each, _, some_pairs, _, some_rows = region(0, prompts, mp_count)
    vmem = pl.BlockSpec(memory_space=pltpu.VMEM)
    dma = pltpu.SemaphoreType.DMA
    return pl.pallas_call(
        functools.partial(combine_kernel, dp_count, mp_count),
        out_shape=jax.ShapeDtypeStruct((prompts, pairs, rows // dp_count, HD), jnp.bfloat16),
        in_specs=[vmem] * 2,
        out_specs=vmem,
        scratch_shapes=[
            pltpu.VMEM(outs.shape, jnp.bfloat16),
            pltpu.VMEM(stats.shape, jnp.float32),
            pltpu.VMEM((count, each, some_pairs, some_rows, HD), jnp.bfloat16),
            pltpu.VMEM((count, each, 8, rows), jnp.float32),
            pltpu.VMEM((rows, count * 8), jnp.float32),
            pltpu.VMEM((prompts, pairs, rows // dp_count, HD), jnp.bfloat16),
            dma((count,)),
            dma((count,)),
            dma((count,)),
            dma((count,)),
            dma((mp_count,)),
            dma((mp_count,)),
        ],
        compiler_params=pltpu.CompilerParams(
            collective_id=1, has_side_effects=True, vmem_limit_bytes=VMEM_LIMIT
        ),
        name="combine",
    )(outs, stats)


def lineage(parents, step, stop):
    beams = parents.shape[2]
    source = jnp.broadcast_to(jnp.arange(beams, dtype=jnp.int32)[None, :], parents.shape[1:])
    for later in range(step, stop, -1):
        choice = source[:, :, None] == jnp.arange(beams, dtype=jnp.int32)
        source = jnp.sum(jnp.where(choice, parents[later][:, None, :], 0), axis=-1)
    return source


def on_device(
    hidden,
    gain,
    w_query,
    w_key,
    w_value,
    query_bias,
    key_bias,
    value_bias,
    w_out,
    prompt_keys,
    prompt_values,
    gen_keys,
    gen_values,
    parents,
):
    beam = lax.axis_index("dp")
    rank = lax.axis_index("mp")
    beams = lax.axis_size("dp")
    mp_count = lax.axis_size("mp")
    steps, prompts = hidden.shape[:2]
    rows = steps * prompts
    per_rank = -(-HEADS // mp_count)

    widened = hidden.reshape(rows, -1).astype(jnp.float32)
    squares = jnp.sum(widened * widened, axis=-1, keepdims=True)
    scaled = (widened * gain).astype(jnp.bfloat16)
    partial = [
        jnp.dot(scaled, weight, preferred_element_type=jnp.float32)
        for weight in (w_query, w_key, w_value)
    ]
    bias = jnp.concatenate([query_bias, key_bias, value_bias]).reshape(HEADS, HD)
    bias = jnp.pad(bias, ((0, per_rank * mp_count - HEADS), (0, 0)))
    projected = exchange(
        *partial, jnp.broadcast_to(squares, (rows, HD)), bias, beams, mp_count, per_rank
    )

    query = projected[:, :QH].reshape(beams, 2, 2, REPEAT, steps, prompts, HD)
    query = query.transpose(5, 1, 0, 2, 4, 3, 6)
    split = jnp.arange(2)
    same = (split[:, None] == split[None, :])[None, None, None, :, None, None, :, None]
    query = jnp.where(same, query[:, :, :, :, :, :, None, :], jnp.bfloat16(0))
    query = query.reshape(prompts, 2, beams * 2 * steps * REPEAT, 2 * HD)

    own = lax.dynamic_index_in_dim(projected, beam, 0, keepdims=False)
    fresh = own[QH:HEADS].reshape(2, KVH, steps, prompts, HD).transpose(0, 3, 2, 1, 4)
    fresh = fresh.reshape(2, prompts, steps, KVH * HD)
    width = gen_keys.shape[2]
    extras = -(-(width + steps) // 16) * 16
    pad = jnp.zeros((prompts, extras - width - steps, KVH * HD), jnp.bfloat16)
    extra_keys = jnp.concatenate([gen_keys[:, 0], fresh[0], pad], axis=1)
    extra_values = jnp.concatenate([gen_values[:, 0], fresh[1], pad], axis=1)

    seen = []
    for step in range(steps):
        anchor = lineage(parents, step, -1) == beam
        columns = [jnp.broadcast_to(anchor[:, :, None], (prompts, beams, width))]
        for source in range(steps):
            if source <= step:
                flag = (lineage(parents, step, source) == beam) & (rank == 0)
            else:
                flag = jnp.zeros((prompts, beams), jnp.bool_)
            columns.append(flag[:, :, None])
        columns.append(jnp.zeros((prompts, beams, extras - width - steps), jnp.bool_))
        seen.append(jnp.concatenate(columns, axis=2))
    mask = jnp.where(jnp.stack(seen, axis=2), jnp.float32(0), jnp.float32(hidden_fill))
    mask = jnp.broadcast_to(
        mask[:, :, None, :, None, :], (prompts, beams, 2, steps, REPEAT, extras)
    ).reshape(prompts, beams * 2 * steps * REPEAT, extras)

    outs, stats = attend(query, prompt_keys, prompt_values, extra_keys, extra_values, mask)
    attended = combine(outs, stats, beams, mp_count)
    attended = attended.reshape(prompts, 2, 2, steps, REPEAT, HD).transpose(3, 0, 1, 2, 4, 5)
    attended = attended.reshape(rows, QH * HD)
    result = jnp.dot(attended, w_out, preferred_element_type=jnp.float32).astype(jnp.bfloat16)
    return result.reshape(steps, prompts, 1, -1)


def solution(mesh):
    return jax.shard_map(
        on_device,
        mesh=mesh,
        in_specs=(
            P(None, "groups", "dp", "mp"),
            P("mp"),
            P("mp", None),
            P("mp", None),
            P("mp", None),
            P(),
            P(),
            P(),
            P(None, "mp"),
            P("groups", ("dp", "mp"), None),
            P("groups", ("dp", "mp"), None),
            P("groups", "dp", "mp", None),
            P("groups", "dp", "mp", None),
            P(None, "groups", None),
        ),
        out_specs=P(None, "groups", "dp", "mp"),
        check_vma=False,
    )
```

time: 381 us -> 90.8 us (0.24)
  blocking collectives: 171 us -> 0 us
  matrix products: 93 us -> 17.7 us
  Pallas kernels: 0 us -> 70.4 us
  local copies, waits for them, and re-layouts: 54.1 us -> 1.42 us
  waiting for transfers between devices: 30.4 us -> 0 us
  other arithmetic: 17.1 us -> 0.47 us
  between operations: 13.6 us -> 0.3 us
    pallas_call x0 -> x3, Pallas kernels: none -> 70.4 us  [the longest x1 23.8 us: exchange(): pl.pallas_call(functools.partial(exchange_kernel, dp_count, mp_count, per...]
    dot_general x14 -> x3, matrix products: 76.8 us -> 9 us  [on_device(): jnp.dot(scaled, weight, preferred_element_type=jnp.float32)]
    pmax x1 -> x0, blocking collectives: 63.8 us -> none  [on_device(): top = lax.pmax(local_top, ('dp', 'mp'))]
    psum x1 -> x0, blocking collectives: 60.2 us -> none  [on_device(): numerator, total = lax.psum((numerator, total), ('dp', 'mp'))]
    reshape x2 -> x3, local copies, waits for them, and re-layouts: 47.5 us -> 0.1 us  [the longest x1 0.06 us: on_device(): attended = attended.reshape(rows, QH * HD)]
    all_gather x8 -> x0, blocking collectives: 47.2 us -> none  [the longest x2 13 us: fork_caches(): lax.all_gather(keys_now[:, None], 'dp', axis=1, tiled=True)]
    psum x3 -> x0, waiting for transfers between devices: 30.4 us -> none  [the longest x1 30.3 us: on_device(): numerator, total = lax.psum((numerator, total), ('dp', 'mp'))]
    reduce_sum x5 -> x3, other arithmetic: 11.1 us -> 0.16 us  [the longest x1 0.11 us: on_device(): squares = jnp.sum(widened * widened, axis=-1, keepdims=True)]
  transfers between devices with their start and end apart: 3 -> 0, of which waited for: 1 -> 0; matrix products, arithmetic and copies ran while one was open for 18% -> 0% of each run, Pallas kernels for 0% -> 0%
where the time goes in v1:
time: 90.8 us; the launch traced here: 90.3 us
  Pallas kernels  70.4 us (78%)
  matrix products  17.7 us (19%)
  local copies, waits for them, and re-layouts  1.42 us (2%)
    pallas_call x1, Pallas kernels, exchange(): pl.pallas_call(functools.partial(exchange_kernel, dp_count, mp_count, per...  23.8 us
    pallas_call x1, Pallas kernels, attend(): pl.pallas_call(attend_kernel, grid=(prompts, pairs), out_shape=(jax.Shape...  23.8 us
    pallas_call x1, Pallas kernels, combine(): pl.pallas_call(functools.partial(combine_kernel, dp_count, mp_count), out...  22.8 us
    dot_general x3, matrix products, on_device(): jnp.dot(scaled, weight, preferred_element_type=jnp.float32)  9 us
    dot_general x1, matrix products, on_device(): jnp.dot(attended, w_out, preferred_element_type=jnp.float32)  8.68 us

profile of v1, /device:TPU:0, one launch (start us, length us, event | category | flops | bytes accessed | tf_op | source)
XLA Modules:
  0.0 90.3 jit_solution(10284768460669241910)
XLA Ops:
  0.0 0.0 copy-start
  0.0 0.0 copy-start.9
  0.0 0.0 copy-start.10
  0.1 8.2 %fusion.8.query_ref = f32[16,4096]{1,0:T(8,128)S(1)} fusion(bf16[2048,4096]{1,0:T(8,128)(2,1)} %param.16, bf16[2,8,1,2048]{3,1,2,0:T(8,128)(2,1)} %param.14, f32[2048]{0:T(1024)} %param.15), kind=kOutput, calls=%fused_computation.13 | convolution fusion | flops 268533760 | bytes 17113088 | tf_op jit(solution)/shard_map/dot_general | solution.py:454
  8.3 0.0 copy-done.3
  8.3 0.0 copy-done.4
  8.3 0.4 fusion.6.key_ref
  8.7 0.4 fusion.4.value_ref
  9.1 0.1 fusion.3
  9.2 0.1 broadcast_in_dim.122
  9.3 0.1 broadcast_in_dim.123.squares_ref
  9.4 0.0 copy-done.10
  9.4 0.0 copy-done.7
  9.4 23.8 %exchange.1 = bf16[4,40,16,128]{3,2,1,0:T(8,128)(2,1)S(1)} custom-call(f32[16,4096]{1,0:T(8,128)S(1)} %fusion.8.query_ref, f32[16,512]{1,0:T(8,128)S(1)} %fusion.6.key_ref, f32[16,512]{1,0:T(8,128)S(1)} %fusion.4.value_ref, f32[16,128]{1,0:T(8,128)S(1)} %broadcast_in_dim.123.squares_ref, f32[40,128]{1,0:T(8,128)S(1)} %maximum_bitcast_fusion.bias_ref), custom_call_target="tpu_custom_call" | custom-call | tf_op jit(solution)/shard_map/exchange/pallas_call | solution.py:149
  33.3 0.1 copy.33
  33.4 0.2 broadcast_in_dim.124
  33.6 0.1 broadcast_in_dim.119
  33.7 0.1 broadcast_select_fusion.query_ref
  33.9 0.1 pad.15.clone
  34.0 0.1 maximum_maximum_fusion.1
  34.1 0.1 broadcast_in_dim.132
  34.3 0.1 broadcast_in_dim.131
  34.4 0.1 pad.9.clone
  34.4 0.1 pad.8.clone
  34.5 0.1 copy.35
  34.6 0.1 broadcast_in_dim.135
  34.7 0.1 add_bitcast_fusion
  34.9 0.0 copy-start.1
  34.9 23.8 %attend.1 = (bf16[8,2,128,128]{3,2,1,0:T(8,128)(2,1)S(1)}, f32[8,8,128]{2,1,0:T(8,128)S(1)}) custom-call(bf16[8,2,128,256]{3,2,1,0:T(8,128)(2,1)S(1)} %broadcast_select_fusion.query_ref, bf16[8,2048,512]{2,1,0:T(8,128)(2,1)} %key_ref.1, bf16[8,2048,512]{2,1,0:T(8,128)(2,1)} %value_ref.1, bf16[8,16,512]{2,1,0:T(8,128)(2,1)S(1)} %get-tuple-element.18.extra_key_ref, ...), custom_call_target="tpu_custom_call" | custom-call | tf_op jit(solution)/shard_map/attend/pallas_call | solution.py:215
  58.7 22.8 %combine.1 = bf16[8,2,32,128]{3,2,1,0:T(8,128)(2,1)S(1)} custom-call(bf16[8,2,128,128]{3,2,1,0:T(8,128)(2,1)S(1)} %get-tuple-element.7.out_in, f32[8,8,128]{2,1,0:T(8,128)S(1)} %get-tuple-element.8.stat_in), custom_call_target="tpu_custom_call" | custom-call | tf_op jit(solution)/shard_map/combine/pallas_call | solution.py:391
  81.6 0.1 reshape.101
  81.6 8.7 %fusion = bf16[2,8,1,2048]{3,1,2,0:T(8,128)(2,1)} fusion(bf16[16,4096]{1,0:T(8,128)(2,1)S(1)} %reshape.101, bf16[4096,2048]{1,0:T(8,128)(2,1)} %param.22), kind=kOutput, calls=%fused_computation.1 | convolution fusion | flops 268468224 | bytes 16973824 | tf_op jit(solution)/shard_map/dot_general | solution.py:500
  (34 shorter events, 0.3 us)
Async XLA Ops:
  0.0 8.3 %copy-start = (bf16[2048,512]{1,0:T(8,128)(2,1)S(1)}, bf16[2048,512]{1,0:T(8,128)(2,1)}, u32[]{:S(2)}) copy-start(bf16[2048,512]{1,0:T(8,128)(2,1)} %param.17) | copy-start | bytes 6291460
  0.0 8.3 %copy-start.3 = (bf16[2,8,1,2048]{3,1,2,0:T(8,128)(2,1)S(1)}, bf16[2,8,1,2048]{3,1,2,0:T(8,128)(2,1)}, u32[]{:S(2)}) copy-start(bf16[2,8,1,2048]{3,1,2,0:T(8,128)(2,1)} %param.14) | copy-start | bytes 196612
  0.0 8.3 %copy-start.4 = (f32[2048]{0:T(1024)S(1)}, f32[2048]{0:T(1024)}, u32[]{:S(2)}) copy-start(f32[2048]{0:T(1024)} %param.15) | copy-start | bytes 24580
  0.0 8.7 %copy-start.2 = (bf16[2048,512]{1,0:T(8,128)(2,1)S(1)}, bf16[2048,512]{1,0:T(8,128)(2,1)}, u32[]{:S(2)}) copy-start(bf16[2048,512]{1,0:T(8,128)(2,1)} %param.18) | copy-start | bytes 6291460
  0.0 9.4 %copy-start.9 = (f32[512]{0:T(512)S(1)}, f32[512]{0:T(512)}, u32[]{:S(2)}) copy-start(f32[512]{0:T(512)} %param.21) | copy-start | bytes 6148
  0.0 9.4 %copy-start.10 = (f32[512]{0:T(512)S(1)}, f32[512]{0:T(512)}, u32[]{:S(2)}) copy-start(f32[512]{0:T(512)} %param.20) | copy-start | bytes 6148
  0.0 9.3 %copy-start.7 = (f32[4096]{0:T(1024)S(1)}, f32[4096]{0:T(1024)}, u32[]{:S(2)}) copy-start(f32[4096]{0:T(1024)} %param.19) | copy-start | bytes 49156
  0.0 33.9 %copy-start.5 = (bf16[8,1,8,512]{3,2,1,0:T(8,128)(2,1)S(1)}, bf16[8,1,8,512]{3,2,1,0:T(8,128)(2,1)}, u32[]{:S(2)}) copy-start(bf16[8,1,8,512]{3,2,1,0:T(8,128)(2,1)} %param.26) | copy-start | bytes 196612
  0.1 33.9 %copy-start.6 = (bf16[8,1,8,512]{3,2,1,0:T(8,128)(2,1)S(1)}, bf16[8,1,8,512]{3,2,1,0:T(8,128)(2,1)}, u32[]{:S(2)}) copy-start(bf16[8,1,8,512]{3,2,1,0:T(8,128)(2,1)} %param.25) | copy-start | bytes 196612
  0.1 34.2 %copy-start.8 = (s32[2,8,4]{1,2,0:T(4,128)S(1)}, s32[2,8,4]{1,2,0:T(4,128)}, u32[]{:S(2)}) copy-start(s32[2,8,4]{1,2,0:T(4,128)} %param.27) | copy-start | bytes 772
  34.9 55.4 %copy-start.1 = (bf16[2048,512]{1,0:T(8,128)(2,1)S(1)}, bf16[2048,512]{1,0:T(8,128)(2,1)}, u32[]{:S(2)}) copy-start(bf16[2048,512]{1,0:T(8,128)(2,1)} %param.17) | copy-start | bytes 6291460

commit v2 on v1

--- a/solution.py
+++ b/solution.py
@@ -171,71 +171,6 @@
     )(query, key, value, squares, bias)
 
 
-def attend_kernel(
-    query_ref, key_ref, value_ref, extra_key_ref, extra_value_ref, mask_ref, out_ref, stat_ref
-):
-    pair = pl.program_id(1)
-    factor = HD ** (-0.5)
-    contract_last = (((1,), (1,)), ((), ()))
-    query = query_ref[0, 0]
-    rows = query.shape[0]
-    scores = lax.dot_general(
-        query, key_ref[0], contract_last, preferred_element_type=jnp.float32
-    )
-    extra = lax.dot_general(
-        query, extra_key_ref[0], contract_last, preferred_element_type=jnp.float32
-    )
-    extra = extra + mask_ref[0]
-    top = jnp.maximum(
-        jnp.max(scores, axis=-1, keepdims=True), jnp.max(extra, axis=-1, keepdims=True)
-    )
-    weights = jnp.exp((scores - top) * factor)
-    extra_weights = jnp.exp((extra - top) * factor)
-    total = jnp.sum(weights, axis=-1, keepdims=True) + jnp.sum(
-        extra_weights, axis=-1, keepdims=True
-    )
-    numerator = jnp.dot(
-        weights.astype(jnp.bfloat16), value_ref[0], preferred_element_type=jnp.float32
-    ) + jnp.dot(
-        extra_weights.astype(jnp.bfloat16), extra_value_ref[0], preferred_element_type=jnp.float32
-    )
-    row = lax.broadcasted_iota(jnp.int32, (rows, HD), 0)
-    second = lax.rem(row // (rows // 8), 2) == 1
-    own = jnp.where(second, numerator[:, HD:], numerator[:, :HD])
-    out_ref[0, 0] = (own / total).astype(jnp.bfloat16)
-    level = top * factor + jnp.log(total)
-    flat = jnp.transpose(jnp.broadcast_to(level, (rows, HD)))
-    stat_ref[0, pl.ds(pair, 1), :] = flat[:1]
-
-
-def attend(query, prompt_keys, prompt_values, extra_keys, extra_values, mask):
-    prompts, pairs, rows, wide = query.shape
-    length = prompt_keys.shape[1]
-    extras = extra_keys.shape[1]
-    return pl.pallas_call(
-        attend_kernel,
-        grid=(prompts, pairs),
-        out_shape=(
-            jax.ShapeDtypeStruct((prompts, pairs, rows, HD), jnp.bfloat16),
-            jax.ShapeDtypeStruct((prompts, 8, rows), jnp.float32),
-        ),
-        in_specs=[
-            pl.BlockSpec((1, 1, rows, wide), lambda p, h: (p, h, 0, 0)),
-            pl.BlockSpec((1, length, wide), lambda p, h: (p, 0, h)),
-            pl.BlockSpec((1, length, wide), lambda p, h: (p, 0, h)),
-            pl.BlockSpec((1, extras, wide), lambda p, h: (p, 0, h)),
-            pl.BlockSpec((1, extras, wide), lambda p, h: (p, 0, h)),
-            pl.BlockSpec((1, rows, extras), lambda p, h: (p, 0, 0)),
-        ],
-        out_specs=(
-            pl.BlockSpec((1, 1, rows, HD), lambda p, h: (p, h, 0, 0)),
-            pl.BlockSpec((1, 8, rows), lambda p, h: (p, 0, 0)),
-        ),
-        compiler_params=pltpu.CompilerParams(vmem_limit_bytes=VMEM_LIMIT),
-        name="attend",
-    )(query, prompt_keys, prompt_values, extra_keys, extra_values, mask)
-
-
 def region(rank, prompts, mp_count):
     if mp_count <= prompts:
         each = prompts // mp_count
@@ -247,18 +182,26 @@
     return rank // share, 1, place // 2, 1, lax.rem(place, 2) * 16, 16
 
 
-def combine_kernel(
+def attend_kernel(
     dp_count,
     mp_count,
-    out_in,
-    stat_in,
+    query_ref,
+    key_hbm,
+    value_hbm,
+    extra_key_ref,
+    extra_value_ref,
+    mask_ref,
     out_ref,
+    keys,
+    values,
     outs,
     stats,
     landed,
     landed_stats,
     flipped,
     gathered,
+    key_sem,
+    value_sem,
     out_send,
     out_recv,
     stat_send,
@@ -270,8 +213,27 @@
     rank = lax.axis_index("mp")
     count = dp_count * mp_count
     me = beam * mp_count + rank
-    prompts = out_in.shape[0]
-    beam_rows = out_in.shape[2] // dp_count
+    prompts, pairs_all, wide_rows, wide = query_ref.shape
+    beam_rows = wide_rows // dp_count
+    share = max(1, mp_count // prompts)
+    each = max(1, prompts // mp_count)
+    factor = HD ** (-0.5)
+    contract_last = (((1,), (1,)), ((), ()))
+    origin = rank * each // share + each
+
+    def place_of(turn):
+        return lax.rem(origin + turn, prompts)
+
+    def loads(turn):
+        prompt = place_of(turn)
+        slot = lax.rem(turn, 2)
+        return (
+            pltpu.make_async_copy(key_hbm.at[prompt], keys.at[slot], key_sem.at[slot]),
+            pltpu.make_async_copy(value_hbm.at[prompt], values.at[slot], value_sem.at[slot]),
+        )
+
+    for copy in loads(0):
+        copy.start()
 
     barrier = pltpu.get_barrier_semaphore()
 
@@ -286,56 +248,131 @@
         return carry
 
     lax.fori_loop(1, count, greet, 0)
-    outs[...] = out_in[...]
-    stats[...] = stat_in[...]
+    stats[...] = jnp.zeros_like(stats)
     pl.semaphore_wait(barrier, count - 1)
 
-    def views(peer):
-        first, each, pair, pairs, row, rows = region(lax.rem(peer, mp_count), prompts, mp_count)
-        start = pl.multiple_of((peer // mp_count) * beam_rows + row, 16)
-        return (
-            outs.at[pl.ds(first, each), pl.ds(pair, pairs), pl.ds(start, rows)],
-            stats.at[pl.ds(first, each)],
-        )
-
-    def copies(delta):
-        peer = lax.rem(me + delta, count)
-        target = {"dp": peer // mp_count, "mp": lax.rem(peer, mp_count)}
-        out_view, stat_view = views(peer)
+    def owner_of(turn, target):
+        prompt = place_of(turn)
+        if share > 1:
+            return prompt * share + lax.rem(target, share)
+        return prompt // each
+
+    def sends(turn, target):
+        prompt = place_of(turn)
+        owner = owner_of(turn, target)
+        other = target // share
+        _, _, pair, pairs, row, rows = region(owner, prompts, mp_count)
+        item = lax.rem(prompt, each)
+        start = pl.multiple_of(other * beam_rows + row, 16)
+        where = {"dp": other, "mp": owner}
         return (
             pltpu.make_async_remote_copy(
-                src_ref=out_view,
-                dst_ref=landed.at[delta],
-                send_sem=out_send.at[delta],
-                recv_sem=out_recv.at[delta],
-                device_id=target,
+                src_ref=outs.at[prompt, pl.ds(pair, pairs), pl.ds(start, rows)],
+                dst_ref=landed.at[me, item],
+                send_sem=out_send.at[turn, target],
+                recv_sem=out_recv.at[me, item],
+                device_id=where,
                 device_id_type=MESH,
             ),
             pltpu.make_async_remote_copy(
-                src_ref=stat_view,
-                dst_ref=landed_stats.at[delta],
-                send_sem=stat_send.at[delta],
-                recv_sem=stat_recv.at[delta],
-                device_id=target,
+                src_ref=stats.at[prompt],
+                dst_ref=landed_stats.at[me, item],
+                send_sem=stat_send.at[turn, target],
+                recv_sem=stat_recv.at[me, item],
+                device_id=where,
                 device_id_type=MESH,
             ),
         )
 
-    def begin(delta, carry):
-        for copy in copies(delta):
-            copy.start()
+    def away(turn, target):
+        return (target // share) * mp_count + owner_of(turn, target) != me
+
+    row_id = lax.broadcasted_iota(jnp.int32, (wide_rows, HD), 0)
+    second = lax.rem(row_id // (wide_rows // 8), 2) == 1
+
+    def work(turn, carry):
+        prompt = place_of(turn)
+        slot = lax.rem(turn, 2)
+
+        @pl.when(turn + 1 < prompts)
+        def _():
+            for copy in loads(turn + 1):
+                copy.start()
+
+        for copy in loads(turn):
+            copy.wait()
+        for pair in range(pairs_all):
+            lanes = slice(pair * wide, (pair + 1) * wide)
+            query = query_ref[prompt, pair]
+            scores = lax.dot_general(
+                query, keys[slot, :, lanes], contract_last, preferred_element_type=jnp.float32
+            )
+            extra = lax.dot_general(
+                query,
+                extra_key_ref[prompt, :, lanes],
+                contract_last,
+                preferred_element_type=jnp.float32,
+            )
+            extra = extra + mask_ref[prompt]
+            top = jnp.maximum(
+                jnp.max(scores, axis=-1, keepdims=True), jnp.max(extra, axis=-1, keepdims=True)
+            )
+            weights = jnp.exp((scores - top) * factor)
+            extra_weights = jnp.exp((extra - top) * factor)
+            total = jnp.sum(weights, axis=-1, keepdims=True) + jnp.sum(
+                extra_weights, axis=-1, keepdims=True
+            )
+            numerator = jnp.dot(
+                weights.astype(jnp.bfloat16),
+                values[slot, :, lanes],
+                preferred_element_type=jnp.float32,
+            ) + jnp.dot(
+                extra_weights.astype(jnp.bfloat16),
+                extra_value_ref[prompt, :, lanes],
+                preferred_element_type=jnp.float32,
+            )
+            own = jnp.where(second, numerator[:, HD:], numerator[:, :HD])
+            outs[prompt, pair] = (own / total).astype(jnp.bfloat16)
+            level = top * factor + jnp.log(total)
+            flat = jnp.transpose(jnp.broadcast_to(level, (wide_rows, HD)))
+            stats[prompt, pair : pair + 1] = flat[:1]
+        for target in range(dp_count * share):
+
+            @pl.when(away(turn, target))
+            def _():
+                for copy in sends(turn, target):
+                    copy.start()
+
         return carry
 
+    lax.fori_loop(0, prompts, work, 0)
+
+    first, _, pair, pairs, row, rows = region(rank, prompts, mp_count)
+    start = pl.multiple_of(beam * beam_rows + row, 16)
+    landed[me] = outs[pl.ds(first, each), pl.ds(pair, pairs), pl.ds(start, rows)]
+    landed_stats[me] = stats[pl.ds(first, each)]
+
     def finish(delta, carry):
-        for copy in copies(delta):
-            copy.wait()
+        peer = lax.rem(me + delta, count)
+        for item in range(each):
+            pltpu.make_async_remote_copy(
+                src_ref=landed.at[me, item],
+                dst_ref=landed.at[peer, item],
+                send_sem=out_send.at[0, 0],
+                recv_sem=out_recv.at[peer, item],
+                device_id={"dp": peer // mp_count, "mp": lax.rem(peer, mp_count)},
+                device_id_type=MESH,
+            ).wait_recv()
+            pltpu.make_async_remote_copy(
+                src_ref=landed_stats.at[me, item],
+                dst_ref=landed_stats.at[peer, item],
+                send_sem=stat_send.at[0, 0],
+                recv_sem=stat_recv.at[peer, item],
+                device_id={"dp": peer // mp_count, "mp": lax.rem(peer, mp_count)},
+                device_id_type=MESH,
+            ).wait_recv()
         return carry
 
-    lax.fori_loop(1, count, begin, 0)
-    first, each, pair, pairs, row, rows = region(rank, prompts, mp_count)
-    start = pl.multiple_of(beam * beam_rows + row, 16)
-    landed[0] = outs[pl.ds(first, each), pl.ds(pair, pairs), pl.ds(start, rows)]
-    landed_stats[0] = stats[pl.ds(first, each)]
     lax.fori_loop(1, count, finish, 0)
 
     for item in range(each):
@@ -379,39 +416,58 @@
         spread(delta).start()
     for delta in range(1, mp_count):
         spread(delta).wait()
+
+    def drain(turn, carry):
+        for target in range(dp_count * share):
+
+            @pl.when(away(turn, target))
+            def _():
+                for copy in sends(turn, target):
+                    copy.wait_send()
+
+        return carry
+
+    lax.fori_loop(0, prompts, drain, 0)
     out_ref[...] = gathered[...]
 
 
-def combine(outs, stats, dp_count, mp_count):
-    prompts, pairs, rows, _ = outs.shape
+def attend(query, prompt_keys, prompt_values, extra_keys, extra_values, mask, dp_count, mp_count):
+    prompts, pairs, rows, _ = query.shape
     count = dp_count * mp_count
     _, each, _, some_pairs, _, some_rows = region(0, prompts, mp_count)
+    targets = dp_count * max(1, mp_count // prompts)
     vmem = pl.BlockSpec(memory_space=pltpu.VMEM)
+    hbm = pl.BlockSpec(memory_space=pl.ANY)
     dma = pltpu.SemaphoreType.DMA
+    merged = (prompts, pairs, rows // dp_count, HD)
     return pl.pallas_call(
-        functools.partial(combine_kernel, dp_count, mp_count),
-        out_shape=jax.ShapeDtypeStruct((prompts, pairs, rows // dp_count, HD), jnp.bfloat16),
-        in_specs=[vmem] * 2,
+        functools.partial(attend_kernel, dp_count, mp_count),
+        out_shape=jax.ShapeDtypeStruct(merged, jnp.bfloat16),
+        in_specs=[vmem, hbm, hbm, vmem, vmem, vmem],
         out_specs=vmem,
         scratch_shapes=[
-            pltpu.VMEM(outs.shape, jnp.bfloat16),
-            pltpu.VMEM(stats.shape, jnp.float32),
+            pltpu.VMEM((2,) + prompt_keys.shape[1:], jnp.bfloat16),
+            pltpu.VMEM((2,) + prompt_values.shape[1:], jnp.bfloat16),
+            pltpu.VMEM((prompts, pairs, rows, HD), jnp.bfloat16),
+            pltpu.VMEM((prompts, 8, rows), jnp.float32),
             pltpu.VMEM((count, each, some_pairs, some_rows, HD), jnp.bfloat16),
             pltpu.VMEM((count, each, 8, rows), jnp.float32),
             pltpu.VMEM((rows, count * 8), jnp.float32),
-            pltpu.VMEM((prompts, pairs, rows // dp_count, HD), jnp.bfloat16),
-            dma((count,)),
-            dma((count,)),
-            dma((count,)),
-            dma((count,)),
+            pltpu.VMEM(merged, jnp.bfloat16),
+            dma((2,)),
+            dma((2,)),
+            dma((prompts, targets)),
+            dma((count, each)),
+            dma((prompts, targets)),
+            dma((count, each)),
             dma((mp_count,)),
             dma((mp_count,)),
         ],
         compiler_params=pltpu.CompilerParams(
             collective_id=1, has_side_effects=True, vmem_limit_bytes=VMEM_LIMIT
         ),
-        name="combine",
-    )(outs, stats)
+        name="attend",
+    )(query, prompt_keys, prompt_values, extra_keys, extra_values, mask)
 
 
 def lineage(parents, step, stop):
@@ -493,8 +549,9 @@
         mask[:, :, None, :, None, :], (prompts, beams, 2, steps, REPEAT, extras)
     ).reshape(prompts, beams * 2 * steps * REPEAT, extras)
 
-    outs, stats = attend(query, prompt_keys, prompt_values, extra_keys, extra_values, mask)
-    attended = combine(outs, stats, beams, mp_count)
+    attended = attend(
+        query, prompt_keys, prompt_values, extra_keys, extra_values, mask, beams, mp_count
+    )
     attended = attended.reshape(prompts, 2, 2, steps, REPEAT, HD).transpose(3, 0, 1, 2, 4, 5)
     attended = attended.reshape(rows, QH * HD)
     result = jnp.dot(attended, w_out, preferred_element_type=jnp.float32).astype(jnp.bfloat16)

time: 90.8 us -> 72.4 us (0.80)
  Pallas kernels: 70.4 us -> 52.4 us
    pallas_call x2 -> x1, Pallas kernels: 46.6 us -> 28.6 us  [attend(): pl.pallas_call(functools.partial(attend_kernel, dp_count, mp_count), out_...]
where the time goes in v2:
time: 72.4 us; the launch traced here: 72.3 us
  Pallas kernels  52.4 us (72%)
  matrix products  17.7 us (24%)
  local copies, waits for them, and re-layouts  1.42 us (2%)
    pallas_call x1, Pallas kernels, attend(): pl.pallas_call(functools.partial(attend_kernel, dp_count, mp_count), out_...  28.6 us
    pallas_call x1, Pallas kernels, exchange(): pl.pallas_call(functools.partial(exchange_kernel, dp_count, mp_count, per...  23.8 us
    dot_general x3, matrix products, on_device(): jnp.dot(scaled, weight, preferred_element_type=jnp.float32)  9 us
    dot_general x1, matrix products, on_device(): jnp.dot(attended, w_out, preferred_element_type=jnp.float32)  8.68 us

profile of v2, /device:TPU:0, one launch (start us, length us, event | category | flops | bytes accessed | tf_op | source)
XLA Modules:
  0.0 72.3 jit_solution(13817074167875986888)
XLA Ops:
  0.0 0.0 copy-start
  0.0 0.0 copy-start.9
  0.0 0.0 copy-start.10
  0.0 0.0 copy-start.7
  0.0 0.0 copy-start.5
  0.1 0.0 copy-start.6
  0.1 8.2 %fusion.8.query_ref = f32[16,4096]{1,0:T(8,128)S(1)} fusion(bf16[2048,4096]{1,0:T(8,128)(2,1)} %param.16, bf16[2,8,1,2048]{3,1,2,0:T(8,128)(2,1)} %param.14, f32[2048]{0:T(1024)} %param.15), kind=kOutput, calls=%fused_computation.13 | convolution fusion | flops 268533760 | bytes 17113088 | tf_op jit(solution)/shard_map/dot_general | solution.py:510
  8.3 0.0 copy-done.4
  8.3 0.4 fusion.6.key_ref
  8.7 0.4 fusion.4.value_ref
  9.1 0.1 fusion.3
  9.2 0.1 broadcast_in_dim.122
  9.3 0.1 broadcast_in_dim.123.squares_ref
  9.4 0.0 copy-done.7
  9.4 23.8 %exchange.1 = bf16[4,40,16,128]{3,2,1,0:T(8,128)(2,1)S(1)} custom-call(f32[16,4096]{1,0:T(8,128)S(1)} %fusion.8.query_ref, f32[16,512]{1,0:T(8,128)S(1)} %fusion.6.key_ref, f32[16,512]{1,0:T(8,128)S(1)} %fusion.4.value_ref, f32[16,128]{1,0:T(8,128)S(1)} %broadcast_in_dim.123.squares_ref, f32[40,128]{1,0:T(8,128)S(1)} %maximum_bitcast_fusion.bias_ref), custom_call_target="tpu_custom_call" | custom-call | tf_op jit(solution)/shard_map/exchange/pallas_call | solution.py:149
  33.3 0.1 copy.33
  33.4 0.2 broadcast_in_dim.124
  33.6 0.1 broadcast_in_dim.119
  33.7 0.1 broadcast_select_fusion.query_ref
  33.9 0.1 pad.15.clone
  34.0 0.1 maximum_maximum_fusion.1
  34.1 0.1 broadcast_in_dim.132
  34.3 0.1 broadcast_in_dim.131
  34.4 0.1 pad.9.clone
  34.4 0.1 pad.8.clone
  34.5 0.1 copy.35
  34.6 0.1 broadcast_in_dim.135
  34.7 0.1 add_bitcast_fusion
  34.9 0.0 copy-start.1
  34.9 28.6 %attend.1 = bf16[8,2,32,128]{3,2,1,0:T(8,128)(2,1)S(1)} custom-call(bf16[8,2,128,256]{3,2,1,0:T(8,128)(2,1)S(1)} %broadcast_select_fusion.query_ref, bf16[8,2048,512]{2,1,0:T(8,128)(2,1)} %key_hbm.1, bf16[8,2048,512]{2,1,0:T(8,128)(2,1)} %value_hbm.1, bf16[8,16,512]{2,1,0:T(8,128)(2,1)S(1)} %get-tuple-element.14.extra_key_ref, ...), custom_call_target="tpu_custom_call" | custom-call | tf_op jit(solution)/shard_map/attend/pallas_call | solution.py:443
  63.5 0.1 reshape.101
  63.6 8.7 %fusion = bf16[2,8,1,2048]{3,1,2,0:T(8,128)(2,1)} fusion(bf16[16,4096]{1,0:T(8,128)(2,1)S(1)} %reshape.101, bf16[4096,2048]{1,0:T(8,128)(2,1)} %param.22), kind=kOutput, calls=%fused_computation.1 | convolution fusion | flops 268468224 | bytes 16973824 | tf_op jit(solution)/shard_map/dot_general | solution.py:557
  (33 shorter events, 0.3 us)
Async XLA Ops:
  0.0 8.3 %copy-start = (bf16[2048,512]{1,0:T(8,128)(2,1)S(1)}, bf16[2048,512]{1,0:T(8,128)(2,1)}, u32[]{:S(2)}) copy-start(bf16[2048,512]{1,0:T(8,128)(2,1)} %param.17) | copy-start | bytes 6291460
  0.0 8.3 %copy-start.3 = (bf16[2,8,1,2048]{3,1,2,0:T(8,128)(2,1)S(1)}, bf16[2,8,1,2048]{3,1,2,0:T(8,128)(2,1)}, u32[]{:S(2)}) copy-start(bf16[2,8,1,2048]{3,1,2,0:T(8,128)(2,1)} %param.14) | copy-start | bytes 196612
  0.0 8.3 %copy-start.4 = (f32[2048]{0:T(1024)S(1)}, f32[2048]{0:T(1024)}, u32[]{:S(2)}) copy-start(f32[2048]{0:T(1024)} %param.15) | copy-start | bytes 24580
  0.0 8.7 %copy-start.2 = (bf16[2048,512]{1,0:T(8,128)(2,1)S(1)}, bf16[2048,512]{1,0:T(8,128)(2,1)}, u32[]{:S(2)}) copy-start(bf16[2048,512]{1,0:T(8,128)(2,1)} %param.18) | copy-start | bytes 6291460
  0.0 9.4 %copy-start.9 = (f32[512]{0:T(512)S(1)}, f32[512]{0:T(512)}, u32[]{:S(2)}) copy-start(f32[512]{0:T(512)} %param.21) | copy-start | bytes 6148
  0.0 9.4 %copy-start.10 = (f32[512]{0:T(512)S(1)}, f32[512]{0:T(512)}, u32[]{:S(2)}) copy-start(f32[512]{0:T(512)} %param.20) | copy-start | bytes 6148
  0.0 9.3 %copy-start.7 = (f32[4096]{0:T(1024)S(1)}, f32[4096]{0:T(1024)}, u32[]{:S(2)}) copy-start(f32[4096]{0:T(1024)} %param.19) | copy-start | bytes 49156
  0.0 33.9 %copy-start.5 = (bf16[8,1,8,512]{3,2,1,0:T(8,128)(2,1)S(1)}, bf16[8,1,8,512]{3,2,1,0:T(8,128)(2,1)}, u32[]{:S(2)}) copy-start(bf16[8,1,8,512]{3,2,1,0:T(8,128)(2,1)} %param.26) | copy-start | bytes 196612
  0.1 33.9 %copy-start.6 = (bf16[8,1,8,512]{3,2,1,0:T(8,128)(2,1)S(1)}, bf16[8,1,8,512]{3,2,1,0:T(8,128)(2,1)}, u32[]{:S(2)}) copy-start(bf16[8,1,8,512]{3,2,1,0:T(8,128)(2,1)} %param.25) | copy-start | bytes 196612
  0.1 34.2 %copy-start.8 = (s32[2,8,4]{1,2,0:T(4,128)S(1)}, s32[2,8,4]{1,2,0:T(4,128)}, u32[]{:S(2)}) copy-start(s32[2,8,4]{1,2,0:T(4,128)} %param.27) | copy-start | bytes 772
  34.9 37.4 %copy-start.1 = (bf16[2048,512]{1,0:T(8,128)(2,1)S(1)}, bf16[2048,512]{1,0:T(8,128)(2,1)}, u32[]{:S(2)}) copy-start(bf16[2048,512]{1,0:T(8,128)(2,1)} %param.17) | copy-start | bytes 6291460

commit v3 on v2

--- a/solution.py
+++ b/solution.py
@@ -12,9 +12,8 @@
 KVH = 4
 HD = 128
 REPEAT = QH // KVH
-HEADS = QH + 2 * KVH
 MESH = pl.DeviceIdType.MESH
-VMEM_LIMIT = 48 * 1024 * 1024
+VMEM_LIMIT = 60 * 1024 * 1024
 hidden_fill = -1e30
 
 
@@ -22,12 +21,19 @@
     dp_count,
     mp_count,
     per_rank,
-    query_ref,
-    key_ref,
-    value_ref,
+    scaled_ref,
+    query_hbm,
+    key_hbm,
+    value_hbm,
     squares_ref,
     bias_ref,
     out_ref,
+    query_slots,
+    key_slots,
+    value_slots,
+    query_sem,
+    key_sem,
+    value_sem,
     parts,
     landed,
     gathered,
@@ -42,9 +48,29 @@
 ):
     beam = lax.axis_index("dp")
     rank = lax.axis_index("mp")
-    rows = squares_ref.shape[0]
     far = lax.rem(beam + dp_count // 2, dp_count)
     near = beam + 1 - 2 * lax.rem(beam, 2)
+
+    slots = query_slots.shape[0]
+    query_width = query_slots.shape[2]
+
+    def weights(step):
+        owner = lax.rem(rank + step + 1, mp_count)
+        narrow = jnp.minimum(owner, KVH - 1)
+        slot = step % slots
+        wide = pl.ds(pl.multiple_of(owner * query_width, HD), query_width)
+        head = pl.ds(pl.multiple_of(narrow * HD, HD), HD)
+        return (
+            pltpu.make_async_copy(
+                query_hbm.at[:, wide], query_slots.at[slot], query_sem.at[slot]
+            ),
+            pltpu.make_async_copy(key_hbm.at[:, head], key_slots.at[slot], key_sem.at[slot]),
+            pltpu.make_async_copy(value_hbm.at[:, head], value_slots.at[slot], value_sem.at[slot]),
+        )
+
+    for step in range(slots):
+        for copy in weights(step):
+            copy.start()
 
     barrier = pltpu.get_barrier_semaphore()
     for delta in range(1, mp_count):
@@ -57,20 +83,6 @@
     for partner in (far, near):
         pl.semaphore_signal(barrier, inc=1, device_id={"dp": partner}, device_id_type=MESH)
 
-    for owner in range(mp_count):
-        for place in range(per_rank):
-            head = owner * per_rank + place
-            if head < QH:
-                part = query_ref[:, head * HD : (head + 1) * HD]
-            elif head < QH + KVH:
-                part = key_ref[:, (head - QH) * HD : (head - QH + 1) * HD]
-            elif head < HEADS:
-                first = (head - QH - KVH) * HD
-                part = value_ref[:, first : first + HD]
-            else:
-                part = jnp.zeros((rows, HD), jnp.float32)
-            parts[owner, place] = part
-        parts[owner, per_rank] = squares_ref[...]
     pl.semaphore_wait(barrier, mp_count + 1)
 
     def reduce_copy(delta):
@@ -84,8 +96,28 @@
             device_id_type=MESH,
         )
 
-    for delta in range(1, mp_count):
-        reduce_copy(delta).start()
+    scaled = scaled_ref[...]
+    places = query_width // HD
+    for step in range(mp_count):
+        owner = lax.rem(rank + step + 1, mp_count)
+        slot = step % slots
+        for copy in weights(step):
+            copy.wait()
+        product = jnp.dot(scaled, query_slots[slot], preferred_element_type=jnp.float32)
+        for place in range(places):
+            parts[owner, place] = product[:, place * HD : (place + 1) * HD]
+        parts[owner, places] = jnp.dot(
+            scaled, key_slots[slot], preferred_element_type=jnp.float32
+        )
+        parts[owner, places + 1] = jnp.dot(
+            scaled, value_slots[slot], preferred_element_type=jnp.float32
+        )
+        parts[owner, per_rank] = squares_ref[...]
+        if step + slots < mp_count:
+            for copy in weights(step + slots):
+                copy.start()
+        if step < mp_count - 1:
+            reduce_copy(step + 1).start()
     total = parts[rank]
     for delta in range(1, mp_count):
         reduce_copy(delta).wait_recv()
@@ -141,17 +173,26 @@
     out_ref[...] = gathered[...]
 
 
-def exchange(query, key, value, squares, bias, dp_count, mp_count, per_rank):
+def exchange(scaled, query, key, value, squares, bias, dp_count, mp_count, per_rank):
     rows = squares.shape[0]
     heads = mp_count * per_rank
+    depth = query.shape[0]
+    slots = min(mp_count, 3)
     vmem = pl.BlockSpec(memory_space=pltpu.VMEM)
+    hbm = pl.BlockSpec(memory_space=pl.ANY)
     dma = pltpu.SemaphoreType.DMA
     return pl.pallas_call(
         functools.partial(exchange_kernel, dp_count, mp_count, per_rank),
         out_shape=jax.ShapeDtypeStruct((dp_count, heads, rows, HD), jnp.bfloat16),
-        in_specs=[vmem] * 5,
+        in_specs=[vmem, hbm, hbm, hbm, vmem, vmem],
         out_specs=vmem,
         scratch_shapes=[
+            pltpu.VMEM((slots, depth, query.shape[1] // mp_count), jnp.bfloat16),
+            pltpu.VMEM((slots, depth, HD), jnp.bfloat16),
+            pltpu.VMEM((slots, depth, HD), jnp.bfloat16),
+            dma((slots,)),
+            dma((slots,)),
+            dma((slots,)),
             pltpu.VMEM((mp_count, per_rank + 1, rows, HD), jnp.float32),
             pltpu.VMEM((mp_count, per_rank + 1, rows, HD), jnp.float32),
             pltpu.VMEM((dp_count, heads, rows, HD), jnp.bfloat16),
@@ -168,7 +209,7 @@
             collective_id=0, has_side_effects=True, vmem_limit_bytes=VMEM_LIMIT
         ),
         name="exchange",
-    )(query, key, value, squares, bias)
+    )(scaled, query, key, value, squares, bias)
 
 
 def region(rank, prompts, mp_count):
@@ -501,22 +542,31 @@
     mp_count = lax.axis_size("mp")
     steps, prompts = hidden.shape[:2]
     rows = steps * prompts
-    per_rank = -(-HEADS // mp_count)
+    per_rank = QH // mp_count + 2
 
     widened = hidden.reshape(rows, -1).astype(jnp.float32)
     squares = jnp.sum(widened * widened, axis=-1, keepdims=True)
     scaled = (widened * gain).astype(jnp.bfloat16)
-    partial = [
-        jnp.dot(scaled, weight, preferred_element_type=jnp.float32)
-        for weight in (w_query, w_key, w_value)
+    places = QH // mp_count
+    narrow = [min(owner, KVH - 1) for owner in range(mp_count)]
+    narrow_bias = [
+        jnp.stack([array[head * HD : (head + 1) * HD] for head in narrow])[:, None]
+        for array in (key_bias, value_bias)
     ]
-    bias = jnp.concatenate([query_bias, key_bias, value_bias]).reshape(HEADS, HD)
-    bias = jnp.pad(bias, ((0, per_rank * mp_count - HEADS), (0, 0)))
+    bias = jnp.concatenate([query_bias.reshape(mp_count, places, HD)] + narrow_bias, axis=1)
     projected = exchange(
-        *partial, jnp.broadcast_to(squares, (rows, HD)), bias, beams, mp_count, per_rank
-    )
-
-    query = projected[:, :QH].reshape(beams, 2, 2, REPEAT, steps, prompts, HD)
+        scaled,
+        w_query,
+        w_key,
+        w_value,
+        jnp.broadcast_to(squares, (rows, HD)),
+        bias.reshape(mp_count * per_rank, HD),
+        beams,
+        mp_count,
+        per_rank,
+    ).reshape(beams, mp_count, per_rank, rows, HD)
+
+    query = projected[:, :, :places].reshape(beams, 2, 2, REPEAT, steps, prompts, HD)
     query = query.transpose(5, 1, 0, 2, 4, 3, 6)
     split = jnp.arange(2)
     same = (split[:, None] == split[None, :])[None, None, None, :, None, None, :, None]
@@ -524,7 +574,7 @@
     query = query.reshape(prompts, 2, beams * 2 * steps * REPEAT, 2 * HD)
 
     own = lax.dynamic_index_in_dim(projected, beam, 0, keepdims=False)
-    fresh = own[QH:HEADS].reshape(2, KVH, steps, prompts, HD).transpose(0, 3, 2, 1, 4)
+    fresh = own[:KVH, places:].reshape(KVH, 2, steps, prompts, HD).transpose(1, 3, 2, 0, 4)
     fresh = fresh.reshape(2, prompts, steps, KVH * HD)
     width = gen_keys.shape[2]
     extras = -(-(width + steps) // 16) * 16

time: 72.4 us -> 81.3 us (1.12)
  matrix products: 17.7 us -> 8.68 us
  local copies, waits for them, and re-layouts: 1.42 us -> 7.92 us
  Pallas kernels: 52.4 us -> 58.8 us
  other arithmetic: 0.47 us -> 5.26 us
    dot_general x3 -> x0, matrix products: 9 us -> none  [on_device(): jnp.dot(scaled, weight, preferred_element_type=jnp.float32)]
    pallas_call x1, Pallas kernels: 28.6 us -> 32 us  [attend(): pl.pallas_call(functools.partial(attend_kernel, dp_count, mp_count), out_...]
    pallas_call x1, Pallas kernels: 23.8 us -> 26.8 us  [exchange(): pl.pallas_call(functools.partial(exchange_kernel, dp_count, mp_count, per...]
    another operation x1 -> x3, local copies, waits for them, and re-layouts: 0.01 us -> 1.67 us  [the longest x2 1.67 us: on_device(): jnp.stack([array[head * HD:(head + 1) * HD] for head in narrow])[:, None]]
    convert_element_type x0 -> x1, other arithmetic: none -> 1.52 us  [on_device(): scaled = (widened * gain).astype(jnp.bfloat16)]
    slice x2, local copies, waits for them, and re-layouts: 0.05 us -> 1.09 us  [the longest x1 1.08 us: on_device(): projected[:, :, :places].reshape(beams, 2, 2, REPEAT, steps, prompts, HD)]
    select_n x1, other arithmetic: 0.07 us -> 1.06 us  [on_device(): query = jnp.where(same, query[:, :, :, :, :, :, None, :], jnp.bfloat16(0))]
    squeeze x0 -> x1, local copies, waits for them, and re-layouts: none -> 0.93 us  [on_device(): own = lax.dynamic_index_in_dim(projected, beam, 0, keepdims=False)]
where the time goes in v3:
time: 81.3 us; the launch traced here: 80.8 us
  Pallas kernels  58.8 us (72%)
  matrix products  8.68 us (11%)
  local copies, waits for them, and re-layouts  7.92 us (10%)
  other arithmetic  5.26 us (6%)
    pallas_call x1, Pallas kernels, attend(): pl.pallas_call(functools.partial(attend_kernel, dp_count, mp_count), out_...  32 us
    pallas_call x1, Pallas kernels, exchange(): pl.pallas_call(functools.partial(exchange_kernel, dp_count, mp_count, per...  26.8 us
    dot_general x1, matrix products, on_device(): jnp.dot(attended, w_out, preferred_element_type=jnp.float32)  8.68 us
    another operation x2, local copies, waits for them, and re-layouts, on_device(): jnp.stack([array[head * HD:(head + 1) * HD] for head in narrow])[:, None]  1.67 us

profile of v3, /device:TPU:0, one launch (start us, length us, event | category | flops | bytes accessed | tf_op | source)
XLA Modules:
  0.0 80.8 jit_solution(11454225120968891597)
XLA Ops:
  0.0 1.5 %fusion.2.scaled_ref = bf16[16,2048]{1,0:T(8,128)(2,1)} fusion(bf16[2,8,1,2048]{3,1,2,0:T(8,128)(2,1)} %param.14, f32[2048]{0:T(1024)} %param.15), kind=kLoop, calls=%fused_computation.8 | loop fusion | flops 98304 | bytes 139264 | tf_op jit(solution)/shard_map/convert_element_type | solution.py:549
  1.5 0.9 %fusion.3 = f32[2,8]{1,0:T(2,128)S(1)} fusion(bf16[2,8,1,2048]{3,1,2,0:T(8,128)(2,1)} %param.14), kind=kLoop, calls=%fused_computation.9 | loop fusion | flops 98288 | bytes 65600 | tf_op jit(solution)/shard_map/reduce_sum | solution.py:548
  2.5 0.1 broadcast_in_dim.128
  2.6 0.7 broadcast_in_dim.129.squares_ref
  3.2 0.8 %slice_bitcast_fusion.6 = (f32[1,128]{1,0:T(1,128)S(1)}, f32[1,128]{1,0:T(1,128)S(1)}, f32[1,128]{1,0:T(1,128)S(1)}, f32[1,128]{1,0:T(1,128)S(1)}) fusion(f32[512]{0:T(512)} %param.21), kind=kLoop, calls=%fused_computation.35 | loop fusion | bytes 4096 | tf_op jit(solution)/shard_map/stack | solution.py:553
  4.1 0.8 %slice_bitcast_fusion.10 = (f32[1,128]{1,0:T(1,128)S(1)}, f32[1,128]{1,0:T(1,128)S(1)}, f32[1,128]{1,0:T(1,128)S(1)}, f32[1,128]{1,0:T(1,128)S(1)}) fusion(f32[512]{0:T(512)} %param.20), kind=kLoop, calls=%fused_computation.39 | loop fusion | bytes 4096 | tf_op jit(solution)/shard_map/stack | solution.py:553
  4.9 0.7 pad_maximum_fusion
  5.6 0.6 reshape.101.bias_ref
  6.2 26.8 %exchange.1 = bf16[4,40,16,128]{3,2,1,0:T(8,128)(2,1)} custom-call(bf16[16,2048]{1,0:T(8,128)(2,1)} %fusion.2.scaled_ref, bf16[2048,4096]{1,0:T(8,128)(2,1)} %query_hbm.1, bf16[2048,512]{1,0:T(8,128)(2,1)} %key_hbm.2, bf16[2048,512]{1,0:T(8,128)(2,1)} %value_hbm.2, f32[16,128]{1,0:T(8,128)} %broadcast_in_dim.129.squares_ref, f32[40,128]{1,0:T(8,128)} %reshape.101.bias_ref), custom_call_target="tpu_custom_call" | custom-call | tf_op jit(solution)/shard_map/exchange/pallas_call | solution.py:184
  33.1 1.1 %slice.60 = bf16[4,4,8,16,128]{4,3,2,1,0:T(8,128)(2,1)S(1)} slice(bf16[4,4,10,16,128]{4,3,2,1,0:T(8,128)(2,1)} %bitcast.69), slice={[0:4], [0:4], [0:8], [0:16], [0:128]} | slice | bytes 1048576 | tf_op jit(solution)/shard_map/slice | solution.py:569
  34.1 0.1 copy.48
  34.3 0.2 broadcast_in_dim.132
  34.5 0.1 broadcast_in_dim.125
  34.6 1.1 %broadcast_select_fusion.query_ref = bf16[8,2,128,256]{3,2,1,0:T(8,128)(2,1)} fusion(bf16[8,2,128,256]{3,2,1,0:T(8,128)(2,1)S(1)} %bitcast.68, pred[128,256]{1,0:T(8,128)(4,1)S(1)} %bitcast.76), kind=kLoop, calls=%fused_computation.2 | loop fusion | flops 524288 | bytes 2129920 | tf_op jit(solution)/shard_map/jit(_where)/select_n | solution.py:573
  35.6 0.9 %dynamic-slice_bitcast_fusion = bf16[4,10,16,128]{3,2,1,0:T(8,128)(2,1)S(1)} fusion(bf16[4,4,10,16,128]{4,3,2,1,0:T(8,128)(2,1)} %bitcast.70, s32[]{:T(128)S(6)} %select_n.29), kind=kLoop, calls=%fused_computation.6 | loop fusion | bytes 327684 | tf_op jit(solution)/shard_map/jit(dynamic_index_in_dim)/squeeze | solution.py:576
  36.6 0.1 pad.15.clone
  36.7 0.0 copy-done
  36.7 0.0 copy-done.1
  36.7 0.8 %maximum_maximum_fusion.1 = (bf16[8,16,512]{2,1,0:T(8,128)(2,1)}, bf16[8,16,512]{2,1,0:T(8,128)(2,1)}) fusion(bf16[8,2,512]{2,1,0:T(2,128)(2,1)S(1)} %squeeze.20, bf16[8,8,512]{2,1,0:T(8,128)(2,1)S(1)} %bitcast.77, bf16[16]{0:T(256)(128)(2,1)S(1)} %pad.15.clone, bf16[8,2,512]{2,1,0:T(2,128)(2,1)S(1)} %squeeze.18, bf16[8,8,512]{2,1,0:T(8,128)(2,1)S(1)} %bitcast.78), kind=kLoop, calls=%fused_computation.11 | loop fusion | flops 720896 | bytes 426016 | tf_op jit(solution)/shard_map/concatenate | solution.py:583
  37.6 0.1 broadcast_in_dim.140
  37.6 0.0 copy-done.2
  37.7 0.1 broadcast_in_dim.139
  37.8 0.1 pad.9.clone
  37.9 0.1 pad.8.clone
  38.0 0.1 copy.42
  38.1 0.1 broadcast_in_dim.143
  38.1 0.1 add_bitcast_fusion
  38.3 0.9 %broadcast_in_dim.146 = f32[8,4,2,2,8,16]{5,4,3,2,1,0:T(8,128)} broadcast(f32[8,4,2,16]{3,2,1,0:T(2,128)S(1)} %copy.43), dimensions={0,1,3,5} | broadcast | bytes 69632 | tf_op jit(solution)/shard_map/broadcast_in_dim | solution.py:598
  39.1 32.0 %attend.1 = bf16[8,2,32,128]{3,2,1,0:T(8,128)(2,1)} custom-call(bf16[8,2,128,256]{3,2,1,0:T(8,128)(2,1)} %broadcast_select_fusion.query_ref, bf16[8,2048,512]{2,1,0:T(8,128)(2,1)} %key_hbm.3, bf16[8,2048,512]{2,1,0:T(8,128)(2,1)} %value_hbm.3, bf16[8,16,512]{2,1,0:T(8,128)(2,1)} %get-tuple-element.22.extra_key_ref, ...), custom_call_target="tpu_custom_call" | custom-call | tf_op jit(solution)/shard_map/attend/pallas_call | solution.py:484
  71.1 0.9 %copy.49 = bf16[8,2,2,2,8,128]{5,4,2,1,0,3:T(8,128)(2,1)S(1)} copy(bf16[8,2,2,2,8,128]{5,4,3,2,1,0:T(8,128)(2,1)} %bitcast.74) | data formatting | bytes 262144 | tf_op jit(solution)/shard_map/reshape | solution.py:605
  72.0 0.1 reshape.107
  72.1 8.7 %fusion = bf16[2,8,1,2048]{3,1,2,0:T(8,128)(2,1)} fusion(bf16[16,4096]{1,0:T(8,128)(2,1)S(1)} %reshape.107, bf16[4096,2048]{1,0:T(8,128)(2,1)} %param.22), kind=kOutput, calls=%fused_computation.1 | convolution fusion | flops 268468224 | bytes 16973824 | tf_op jit(solution)/shard_map/dot_general | solution.py:607
  (22 shorter events, 0.2 us)
Async XLA Ops:
  0.0 36.7 %copy-start = (bf16[8,1,8,512]{3,2,1,0:T(8,128)(2,1)S(1)}, bf16[8,1,8,512]{3,2,1,0:T(8,128)(2,1)}, u32[]{:S(2)}) copy-start(bf16[8,1,8,512]{3,2,1,0:T(8,128)(2,1)} %param.26) | copy-start | bytes 196612
  0.0 36.7 %copy-start.1 = (bf16[8,1,8,512]{3,2,1,0:T(8,128)(2,1)S(1)}, bf16[8,1,8,512]{3,2,1,0:T(8,128)(2,1)}, u32[]{:S(2)}) copy-start(bf16[8,1,8,512]{3,2,1,0:T(8,128)(2,1)} %param.25) | copy-start | bytes 196612
  0.0 37.6 %copy-start.2 = (s32[2,8,4]{1,2,0:T(4,128)S(1)}, s32[2,8,4]{1,2,0:T(4,128)}, u32[]{:S(2)}) copy-start(s32[2,8,4]{1,2,0:T(4,128)} %param.27) | copy-start | bytes 772

commit v4 on v3

--- a/solution.py
+++ b/solution.py
@@ -13,7 +13,7 @@
 HD = 128
 REPEAT = QH // KVH
 MESH = pl.DeviceIdType.MESH
-VMEM_LIMIT = 60 * 1024 * 1024
+VMEM_LIMIT = 48 * 1024 * 1024
 hidden_fill = -1e30
 
 

time: 81.3 us -> 74.1 us (0.911)
  Pallas kernels: 58.8 us -> 55.6 us
  other arithmetic: 5.26 us -> 2.94 us
  local copies, waits for them, and re-layouts: 7.92 us -> 6.25 us
    unnamed x6 -> x10, local copies, waits for them, and re-layouts: 0.01 us -> 3.19 us
    pallas_call x1, Pallas kernels: 32 us -> 30.1 us  [attend(): pl.pallas_call(functools.partial(attend_kernel, dp_count, mp_count), out_...]
    pallas_call x1, Pallas kernels: 26.8 us -> 25.5 us  [exchange(): pl.pallas_call(functools.partial(exchange_kernel, dp_count, mp_count, per...]
    slice x1, local copies, waits for them, and re-layouts: 1.08 us -> 0.06 us  [on_device(): projected[:, :, :places].reshape(beams, 2, 2, REPEAT, steps, prompts, HD)]
    select_n x1, other arithmetic: 1.06 us -> 0.07 us  [on_device(): query = jnp.where(same, query[:, :, :, :, :, :, None, :], jnp.bfloat16(0))]
    squeeze x1, local copies, waits for them, and re-layouts: 0.93 us -> 0.02 us  [on_device(): own = lax.dynamic_index_in_dim(projected, beam, 0, keepdims=False)]
    reshape x1, local copies, waits for them, and re-layouts: 0.93 us -> 0.02 us  [on_device(): attended.reshape(prompts, 2, 2, steps, REPEAT, HD)]
    broadcast_in_dim x1, local copies, waits for them, and re-layouts: 0.86 us -> 0.04 us  [on_device(): jnp.broadcast_to(mask[:, :, None, :, None, :], (prompts, beams, 2, steps,...]
where the time goes in v4:
time: 74.1 us; the launch traced here: 73.7 us
  Pallas kernels  55.6 us (75%)
  matrix products  8.68 us (12%)
  local copies, waits for them, and re-layouts  6.25 us (8%)
  other arithmetic  2.94 us (4%)
    pallas_call x1, Pallas kernels, attend(): pl.pallas_call(functools.partial(attend_kernel, dp_count, mp_count), out_...  30.1 us
    pallas_call x1, Pallas kernels, exchange(): pl.pallas_call(functools.partial(exchange_kernel, dp_count, mp_count, per...  25.5 us
    dot_general x1, matrix products, on_device(): jnp.dot(attended, w_out, preferred_element_type=jnp.float32)  8.68 us
    unnamed x10, local copies, waits for them, and re-layouts  3.19 us
    another operation x2, local copies, waits for them, and re-layouts, on_device(): jnp.stack([array[head * HD:(head + 1) * HD] for head in narrow])[:, None]  1.67 us

profile of v4, /device:TPU:0, one launch (start us, length us, event | category | flops | bytes accessed | tf_op | source)
XLA Modules:
  0.0 73.7 jit_solution(16498816170581028065)
XLA Ops:
  0.0 0.0 copy-start.2
  0.0 0.9 %fusion.2.scaled_ref = bf16[16,2048]{1,0:T(8,128)(2,1)S(1)} fusion(bf16[2,8,1,2048]{3,1,2,0:T(8,128)(2,1)} %param.14, f32[2048]{0:T(1024)} %param.15), kind=kLoop, calls=%fused_computation.8 | loop fusion | flops 98304 | bytes 139264 | tf_op jit(solution)/shard_map/convert_element_type | solution.py:549
  0.9 0.9 %fusion.3 = f32[2,8]{1,0:T(2,128)S(1)} fusion(bf16[2,8,1,2048]{3,1,2,0:T(8,128)(2,1)} %param.14), kind=kLoop, calls=%fused_computation.9 | loop fusion | flops 98288 | bytes 65600 | tf_op jit(solution)/shard_map/reduce_sum | solution.py:548
  1.8 0.1 broadcast_in_dim.128
  1.9 0.1 broadcast_in_dim.129.squares_ref
  2.0 0.8 %slice_bitcast_fusion.6 = (f32[1,128]{1,0:T(1,128)S(1)}, f32[1,128]{1,0:T(1,128)S(1)}, f32[1,128]{1,0:T(1,128)S(1)}, f32[1,128]{1,0:T(1,128)S(1)}) fusion(f32[512]{0:T(512)} %param.21), kind=kLoop, calls=%fused_computation.35 | loop fusion | bytes 4096 | tf_op jit(solution)/shard_map/stack | solution.py:553
  2.8 0.8 %slice_bitcast_fusion.10 = (f32[1,128]{1,0:T(1,128)S(1)}, f32[1,128]{1,0:T(1,128)S(1)}, f32[1,128]{1,0:T(1,128)S(1)}, f32[1,128]{1,0:T(1,128)S(1)}) fusion(f32[512]{0:T(512)} %param.20), kind=kLoop, calls=%fused_computation.39 | loop fusion | bytes 4096 | tf_op jit(solution)/shard_map/stack | solution.py:553
  3.7 0.7 pad_maximum_fusion
  4.4 0.0 copy-start
  4.4 1.6 %copy-done = bf16[2048,512]{1,0:T(8,128)(2,1)S(1)} copy-done((bf16[2048,512]{1,0:T(8,128)(2,1)S(1)}, bf16[2048,512]{1,0:T(8,128)(2,1)}, u32[]{:S(2)}) %copy-start) | copy-done | bytes 2097176
  6.0 1.6 %copy-done.1 = bf16[2048,512]{1,0:T(8,128)(2,1)S(1)} copy-done((bf16[2048,512]{1,0:T(8,128)(2,1)S(1)}, bf16[2048,512]{1,0:T(8,128)(2,1)}, u32[]{:S(2)}) %copy-start.1) | copy-done | bytes 2097176
  7.6 25.5 %exchange.1 = bf16[4,40,16,128]{3,2,1,0:T(8,128)(2,1)S(1)} custom-call(bf16[16,2048]{1,0:T(8,128)(2,1)S(1)} %fusion.2.scaled_ref, bf16[2048,4096]{1,0:T(8,128)(2,1)} %query_hbm.1, bf16[2048,512]{1,0:T(8,128)(2,1)S(1)} %copy-done, bf16[2048,512]{1,0:T(8,128)(2,1)S(1)} %copy-done.1, f32[16,128]{1,0:T(8,128)S(1)} %broadcast_in_dim.129.squares_ref, ...), custom_call_target="tpu_custom_call" | custom-call | tf_op jit(solution)/shard_map/exchange/pallas_call | solution.py:184
  33.1 0.1 slice.60
  33.2 0.1 copy.48
  33.3 0.2 broadcast_in_dim.132
  33.5 0.1 broadcast_in_dim.125
  33.6 0.1 broadcast_select_fusion.query_ref
  33.8 0.1 pad.15.clone
  33.9 0.0 copy-done.2
  33.9 0.0 copy-done.3
  33.9 0.1 maximum_maximum_fusion.1
  34.0 0.1 broadcast_in_dim.140
  34.1 0.0 copy-done.4
  34.2 0.1 broadcast_in_dim.139
  34.3 0.1 pad.9.clone
  34.3 0.1 pad.8.clone
  34.4 0.1 copy.42
  34.5 0.1 broadcast_in_dim.143
  34.6 0.1 add_bitcast_fusion
  34.8 30.1 %attend.1 = bf16[8,2,32,128]{3,2,1,0:T(8,128)(2,1)S(1)} custom-call(bf16[8,2,128,256]{3,2,1,0:T(8,128)(2,1)S(1)} %broadcast_select_fusion.query_ref, bf16[8,2048,512]{2,1,0:T(8,128)(2,1)} %key_hbm.3, bf16[8,2048,512]{2,1,0:T(8,128)(2,1)} %value_hbm.3, bf16[8,16,512]{2,1,0:T(8,128)(2,1)S(1)} %get-tuple-element.22.extra_key_ref, ...), custom_call_target="tpu_custom_call" | custom-call | tf_op jit(solution)/shard_map/attend/pallas_call | solution.py:484
  64.9 0.1 reshape.107
  65.0 8.7 %fusion = bf16[2,8,1,2048]{3,1,2,0:T(8,128)(2,1)} fusion(bf16[16,4096]{1,0:T(8,128)(2,1)S(1)} %reshape.107, bf16[4096,2048]{1,0:T(8,128)(2,1)} %param.22), kind=kOutput, calls=%fused_computation.1 | convolution fusion | flops 268468224 | bytes 16973824 | tf_op jit(solution)/shard_map/dot_general | solution.py:607
  (26 shorter events, 0.3 us)
Async XLA Ops:
  0.0 33.9 %copy-start.2 = (bf16[8,1,8,512]{3,2,1,0:T(8,128)(2,1)S(1)}, bf16[8,1,8,512]{3,2,1,0:T(8,128)(2,1)}, u32[]{:S(2)}) copy-start(bf16[8,1,8,512]{3,2,1,0:T(8,128)(2,1)} %param.26) | copy-start | bytes 196612
  0.0 33.9 %copy-start.3 = (bf16[8,1,8,512]{3,2,1,0:T(8,128)(2,1)S(1)}, bf16[8,1,8,512]{3,2,1,0:T(8,128)(2,1)}, u32[]{:S(2)}) copy-start(bf16[8,1,8,512]{3,2,1,0:T(8,128)(2,1)} %param.25) | copy-start | bytes 196612
  0.0 34.1 %copy-start.4 = (s32[2,8,4]{1,2,0:T(4,128)S(1)}, s32[2,8,4]{1,2,0:T(4,128)}, u32[]{:S(2)}) copy-start(s32[2,8,4]{1,2,0:T(4,128)} %param.27) | copy-start | bytes 772
  4.4 1.6 %copy-start = (bf16[2048,512]{1,0:T(8,128)(2,1)S(1)}, bf16[2048,512]{1,0:T(8,128)(2,1)}, u32[]{:S(2)}) copy-start(bf16[2048,512]{1,0:T(8,128)(2,1)} %key_hbm.2) | copy-start | bytes 6291460
  6.0 1.6 %copy-start.1 = (bf16[2048,512]{1,0:T(8,128)(2,1)S(1)}, bf16[2048,512]{1,0:T(8,128)(2,1)}, u32[]{:S(2)}) copy-start(bf16[2048,512]{1,0:T(8,128)(2,1)} %value_hbm.2) | copy-start | bytes 6291460
